TPU v7x, 256 devices: a whole 4x4x8 slice. The times are simulated.
256 devices in a mesh: group: 32 (over x, y, core), tp: 8 (over z).
Axes of the slice: x: 4, y: 4, z: 8, core: 2. Of those that a mesh axis runs over, the one named last changes fastest.
Arguments:
- queries_nope: bfloat16 [2, 8192, 8192], P(None, 'group', 'tp'), may hold values from -6 to 6
- queries_rope: bfloat16 [2, 8192, 4096], P(None, 'group', 'tp'), may hold values from -8 to 8
- w_key: bfloat16 [2, 64, 128, 512], P(None, 'tp'), may hold values from -0.5 to 0.5
- w_value: bfloat16 [2, 64, 512, 128], P(None, 'tp'), may hold values from -2.5 to 2.5
- suffix_latent: bfloat16 [2, 8192, 512], P(None, ('group', 'tp')), may hold values from -6 to 6
- suffix_rope: bfloat16 [2, 8192, 64], P(None, ('group', 'tp')), may hold values from -6 to 6
- pool_latent: bfloat16 [2, 512, 64, 512], P(None, 'group'), may hold values from -8 to 8
- pool_rope: bfloat16 [2, 512, 4096], P(None, 'group'), may hold values from -8 to 8
- block_holders: int32 [32, 2, 16], replicated, may hold values from 0 to 31, as said below
- block_ids: int32 [32, 2, 16], replicated, may hold values from 0 to 15
- prefix_blocks: int32 [32, 2], replicated, may hold values from 8 to 16, as said below
Outputs:
- attn_out: bfloat16 [2, 8192, 8192], P(None, 'group', 'tp')
Inputs may be any that keep to these rules, and one draw needn't show every extreme that they name: `block_holders`: no entry names the request's own group; at most 2 entries of one group's lists name one holding group, and in every group's lists some holding group is named exactly 2 times. `prefix_blocks`: some request uses all 16 blocks.
All inputs are finite; a program needn't handle non-finite values.
Results may differ from a plain program's by a relative error of at most 0.014.
Values may be sent and summed in bfloat16 or wider, within the bound.
A program may use at most 128 MiB of HBM per device.

v0:
```python
import math

import jax
import jax.numpy as jnp
from jax import lax
from jax.sharding import PartitionSpec as P


def slot_tables(block_holders, block_ids, groups, own_group, capacity):
    slot_count = block_holders.shape[1] * block_holders.shape[2]
    holders = block_holders.reshape(groups, slot_count)
    block_list = block_ids.reshape(groups, slot_count)
    slot_order = jnp.arange(slot_count, dtype=jnp.int32)
    earlier = slot_order[None, :] < slot_order[:, None]
    same_holder = holders[:, :, None] == holders[:, None, :]
    ranks = jnp.sum((same_holder & earlier[None]).astype(jnp.int32), axis=2)
    chosen = (holders == own_group)[:, :, None] & (
        ranks[:, :, None] == jnp.arange(capacity, dtype=jnp.int32)[None, None, :]
    )
    send_ids = jnp.sum(jnp.where(chosen, block_list[:, :, None], 0), axis=1)
    own_holders = lax.dynamic_index_in_dim(holders, own_group, 0, keepdims=False)
    own_ranks = lax.dynamic_index_in_dim(ranks, own_group, 0, keepdims=False)
    places = own_holders * capacity + own_ranks
    return (send_ids, places)


def fetch_blocks(latent_pool, rope_pool, send_ids, places, groups, capacity):
    flat_ids = send_ids.reshape(-1)
    latent_out = jnp.take(latent_pool, flat_ids, axis=0).reshape(
        (groups, capacity) + latent_pool.shape[1:]
    )
    rope_out = jnp.take(rope_pool, flat_ids, axis=0).reshape(
        (groups, capacity) + rope_pool.shape[1:]
    )
    latent_in, rope_in = (
        lax.all_to_all(latent_out, "group", split_axis=0, concat_axis=0, tiled=True),
        lax.all_to_all(rope_out, "group", split_axis=0, concat_axis=0, tiled=True),
    )
    latent_rows = jnp.take(
        latent_in.reshape((groups * capacity,) + latent_pool.shape[1:]), places, axis=0
    )
    rope_rows = jnp.take(
        rope_in.reshape((groups * capacity,) + rope_pool.shape[1:]), places, axis=0
    )
    return (latent_rows, rope_rows)


def per_device(
    queries_nope,
    queries_rope,
    w_key,
    w_value,
    suffix_latent,
    suffix_rope,
    pool_latent,
    pool_rope,
    block_holders,
    block_ids,
    prefix_blocks,
):
    groups = lax.axis_size("group")
    own_group = lax.axis_index("group")
    requests = block_holders.shape[1]
    blocks = block_holders.shape[2]
    capacity = max(2, (requests * blocks + groups - 2) // (groups - 1))
    send_ids, places = slot_tables(block_holders, block_ids, groups, own_group, capacity)
    counts = lax.dynamic_index_in_dim(prefix_blocks, own_group, 0, keepdims=False)
    suffix_lat, suffix_rp = (
        lax.all_gather(suffix_latent, "tp", axis=1, tiled=True),
        lax.all_gather(suffix_rope, "tp", axis=1, tiled=True),
    )
    layers = queries_nope.shape[0]
    tokens = queries_nope.shape[1]
    suffix_len = tokens // requests
    head_count = w_key.shape[1]
    nope_width = w_key.shape[2]
    latent = w_key.shape[3]
    rope_width = suffix_rope.shape[2]
    block_len = pool_latent.shape[2]
    score_scale = 1.0 / math.sqrt(nope_width + rope_width)
    prefix_len = blocks * block_len
    positions = jnp.arange(prefix_len + suffix_len, dtype=jnp.int32)
    query_rows = jnp.arange(suffix_len, dtype=jnp.int32)
    live_suffix = (positions[None, :] >= prefix_len) & (
        positions[None, :] - prefix_len <= query_rows[:, None]
    )
    results = []
    for layer_index in range(layers):
        latent_rows, rope_rows = fetch_blocks(
            pool_latent[layer_index], pool_rope[layer_index], send_ids, places, groups, capacity
        )
        latent_rows = latent_rows.reshape(requests, prefix_len, latent)
        rope_rows = rope_rows.reshape(requests, prefix_len, rope_width)
        nope_rows = queries_nope[layer_index].reshape(tokens, head_count, nope_width)
        absorbed = jnp.einsum(
            "thn,hnc->thc", nope_rows, w_key[layer_index], preferred_element_type=jnp.float32
        ).astype(jnp.bfloat16)
        rope_query = queries_rope[layer_index].reshape(tokens, head_count, rope_width)
        pieces = []
        for request in range(requests):
            first_row = request * suffix_len
            keys_latent = jnp.concatenate(
                [latent_rows[request], suffix_lat[layer_index, first_row : first_row + suffix_len]],
                axis=0,
            )
            keys_rope = jnp.concatenate(
                [rope_rows[request], suffix_rp[layer_index, first_row : first_row + suffix_len]],
                axis=0,
            )
            scores = jnp.einsum(
                "shc,kc->shk",
                absorbed[first_row : first_row + suffix_len],
                keys_latent,
                preferred_element_type=jnp.float32,
            )
            scores = scores + jnp.einsum(
                "shd,kd->shk",
                rope_query[first_row : first_row + suffix_len],
                keys_rope,
                preferred_element_type=jnp.float32,
            )
            scores = scores * score_scale
            live_prefix = (positions < prefix_len) & (positions // block_len < counts[request])
            live_keys = (live_prefix[None, :] | live_suffix)[:, None, :]
            attention = jax.nn.softmax(jnp.where(live_keys, scores, -jnp.inf), axis=-1).astype(
                jnp.bfloat16
            )
            context = jnp.einsum(
                "shk,kc->shc", attention, keys_latent, preferred_element_type=jnp.float32
            ).astype(jnp.bfloat16)
            heads_out = jnp.einsum(
                "shc,hcv->shv", context, w_value[layer_index], preferred_element_type=jnp.float32
            ).astype(jnp.bfloat16)
            pieces.append(heads_out.reshape(suffix_len, head_count * heads_out.shape[2]))
        results.append(jnp.concatenate(pieces, axis=0))
    return jnp.stack(results)


def solution(mesh):
    in_specs = (
        P(None, "group", "tp"),
        P(None, "group", "tp"),
        P(None, "tp", None, None),
        P(None, "tp", None, None),
        P(None, ("group", "tp"), None),
        P(None, ("group", "tp"), None),
        P(None, "group", None, None),
        P(None, "group", None),
        P(),
        P(),
        P(),
    )
    out_specs = P(None, "group", "tp")
    return jax.shard_map(
        per_device, mesh=mesh, in_specs=in_specs, out_specs=out_specs, check_vma=False
    )
```

profile of v0, /device:TPU:8, one launch (start us, length us, event | category | flops | bytes accessed | tf_op | source)
XLA Modules:
  0.0 253.1 jit_solution(15651217981587876409)
XLA Ops:
  4.2 1.0 slice_bitcast_fusion.7
  7.1 1.1 reshape.237
  8.2 7.5 %all-to-all-start.1 = ((bf16[32,2,4096]{2,1,0:T(2,128)(2,1)}), bf16[32,2,4096]{2,1,0:T(2,128)(2,1)S(1)}, u32[]{:S(2)}, u32[]{:S(2)}) async-start(bf16[32,2,4096]{2,1,0:T(2,128)(2,1)} %reshape.237), calls=%async_computation.1 | async-start | bytes 1048576 | tf_op jit(solution)/shard_map/all_to_all | solution.py:37
  15.8 1.7 slice_bitcast_fusion.1
  17.5 2.9 %gather_fusion.4 = bf16[64,64,512]{2,1,0:T(8,128)(2,1)} fusion(bf16[16,64,512]{2,1,0:T(8,128)(2,1)S(1)} %get-tuple-element.14, s32[1024]{0:T(1024)S(1)} %pad_clamp_fusion.1), kind=kCustom, calls=%fused_computation.4.clone | custom fusion | bytes 8388864 | tf_op jit(solution)/shard_map/jit(_take)/gather | solution.py:29
  20.3 2.8 %gather_fusion = bf16[64,64,512]{2,1,0:T(8,128)(2,1)} fusion(bf16[16,64,512]{2,1,0:T(8,128)(2,1)S(1)} %get-tuple-element.13, s32[1024]{0:T(1024)S(1)} %pad_clamp_fusion.1), kind=kCustom, calls=%fused_computation.clone | custom fusion | bytes 8388864 | tf_op jit(solution)/shard_map/jit(_take)/gather | solution.py:29
  23.2 1.1 reshape.243
  24.3 1.6 all-to-all-done.1
  25.9 5.8 %all-to-all-start.3 = ((bf16[32,2,4096]{2,1,0:T(2,128)(2,1)}), bf16[32,2,4096]{2,1,0:T(2,128)(2,1)S(1)}, u32[]{:S(2)}, u32[]{:S(2)}) async-start(bf16[32,2,4096]{2,1,0:T(2,128)(2,1)} %reshape.243), calls=%async_computation.3 | async-start | bytes 1048576 | tf_op jit(solution)/shard_map/all_to_all | solution.py:37
  31.7 5.9 %broadcast_select_fusion.1 = (bf16[64,64,512]{2,1,0:T(8,128)(2,1)}, bf16[64,64,512]{2,1,0:T(8,128)(2,1)}) fusion(bf16[64,64,512]{2,1,0:T(8,128)(2,1)} %gather_fusion, pred[64]{0:T(512)(128)(4,1)S(1)} %compare_and_fusion.1, bf16[64,64,512]{2,1,0:T(8,128)(2,1)} %gather_fusion.4), kind=kLoop, calls=%fused_computation.37 | loop fusion | flops 4194304 | bytes 16777280 | tf_op jit(solution)/shard_map/jit(_take)/select_n | solution.py:29
  37.7 4.2 %all-to-all-done.3 = bf16[32,2,4096]{2,1,0:T(2,128)(2,1)S(1)} async-done(((bf16[32,2,4096]{2,1,0:T(2,128)(2,1)}), bf16[32,2,4096]{2,1,0:T(2,128)(2,1)S(1)}, u32[]{:S(2)}, u32[]{:S(2)}) %all-to-all-start.3) | async-done | bytes 524320 | tf_op jit(solution)/shard_map/all_to_all | solution.py:37
  42.7 5.7 %all-to-all-start.2 = ((bf16[32,2,64,512]{3,2,1,0:T(8,128)(2,1)}), bf16[32,2,64,512]{3,2,1,0:T(8,128)(2,1)}, u32[]{:S(2)}, u32[]{:S(2)}) async-start(bf16[32,2,64,512]{3,2,1,0:T(8,128)(2,1)} %bitcast.149), calls=%async_computation.2 | async-start | bytes 8388608 | tf_op jit(solution)/shard_map/all_to_all | solution.py:36
  49.2 28.2 %all_gather.7 = bf16[2,256,64]{2,0,1:T(2,128)(2,1)S(1)} all-gather(bf16[2,32,64]{2,0,1:T(2,128)(2,1)S(1)} %copy.156), channel_id=1, replica_groups=mesh['group'=32,'tp'=8] {'tp'}, dimensions={1}, use_global_device_ids=true | all-gather | bytes 73728 | tf_op jit(solution)/shard_map/all_gather | solution.py:70
  79.0 2.1 fusion.99
  84.7 1.3 copy.201
  89.7 25.7 %all_gather.6 = bf16[2,256,512]{2,1,0:T(8,128)(2,1)S(1)} all-gather(bf16[2,32,512]{2,1,0:T(8,128)(2,1)} %param.23), channel_id=1, replica_groups=mesh['group'=32,'tp'=8] {'tp'}, dimensions={1}, use_global_device_ids=true | all-gather | bytes 589824 | tf_op jit(solution)/shard_map/all_gather | solution.py:69
  116.2 2.1 convert_bitcast_fusion.1
  118.3 7.7 %all-to-all-start = ((bf16[32,2,64,512]{3,2,1,0:T(8,128)(2,1)}), bf16[32,2,64,512]{3,2,1,0:T(8,128)(2,1)}, u32[]{:S(2)}, u32[]{:S(2)}) async-start(bf16[32,2,64,512]{3,2,1,0:T(8,128)(2,1)} %bitcast.148), calls=%async_computation | async-start | bytes 8388608 | tf_op jit(solution)/shard_map/all_to_all | solution.py:36
  126.7 2.0 convert_bitcast_fusion
  128.8 1.2 reshape.238
  130.8 1.2 reshape.244
  134.6 2.9 %fusion.51 = f32[1152,128,8]{0,1,2:T(8,128)} fusion(bf16[128,8,64]{0,2,1:T(8,128)(2,1)S(1)} %bitcast.160, bf16[128,64]{0,1:T(8,128)(2,1)S(1)} %bitcast.168, bf16[1024,64]{0,1:T(8,128)(2,1)S(1)} %copy.158), kind=kOutput, calls=%fused_computation.93 | convolution fusion | flops 151289856 | bytes 4997120 | tf_op jit(solution)/shard_map/shd,kd->shk/dot_general | solution.py:116
  137.5 3.1 %fusion.54 = f32[1152,128,8]{0,1,2:T(8,128)} fusion(bf16[128,8,64]{0,2,1:T(8,128)(2,1)S(1)} %bitcast.161, bf16[128,64]{0,1:T(8,128)(2,1)S(1)} %bitcast.169, bf16[1024,64]{0,1:T(8,128)(2,1)S(1)} %copy.164), kind=kOutput, calls=%fused_computation.97 | convolution fusion | flops 151289856 | bytes 4997120 | tf_op jit(solution)/shard_map/shd,kd->shk/dot_general | solution.py:116
  140.6 3.0 %fusion.57 = f32[1152,128,8]{0,1,2:T(8,128)} fusion(bf16[128,8,64]{0,2,1:T(8,128)(2,1)S(1)} %bitcast.162, bf16[128,64]{0,1:T(8,128)(2,1)S(1)} %bitcast.170, bf16[1024,64]{0,1:T(8,128)(2,1)S(1)} %copy.174), kind=kOutput, calls=%fused_computation.101 | convolution fusion | flops 151289856 | bytes 4997120 | tf_op jit(solution)/shard_map/shd,kd->shk/dot_general | solution.py:116
  143.6 3.0 %fusion.60 = f32[1152,128,8]{0,1,2:T(8,128)} fusion(bf16[128,8,64]{0,2,1:T(8,128)(2,1)S(1)} %bitcast.163, bf16[128,64]{0,1:T(8,128)(2,1)S(1)} %bitcast.171, bf16[1024,64]{0,1:T(8,128)(2,1)S(1)} %copy.180), kind=kOutput, calls=%fused_computation.105 | convolution fusion | flops 151289856 | bytes 4997120 | tf_op jit(solution)/shard_map/shd,kd->shk/dot_general | solution.py:116
  146.5 4.2 %gather_fusion.5 = bf16[32,64,512]{2,1,0:T(8,128)(2,1)} fusion(bf16[64,64,512]{2,1,0:T(8,128)(2,1)} %bitcast.37, s32[1024]{0:T(1024)S(1)} %pad_clamp_fusion), kind=kCustom, calls=%fused_computation.5.clone | custom fusion | bytes 4194432 | tf_op jit(solution)/shard_map/jit(_take)/gather | solution.py:39
  150.7 29.6 %all-to-all-done = bf16[32,2,64,512]{3,2,1,0:T(8,128)(2,1)} async-done(((bf16[32,2,64,512]{3,2,1,0:T(8,128)(2,1)}), bf16[32,2,64,512]{3,2,1,0:T(8,128)(2,1)}, u32[]{:S(2)}, u32[]{:S(2)}) %all-to-all-start) | async-done | bytes 4194336 | tf_op jit(solution)/shard_map/all_to_all | solution.py:36
  180.3 4.2 %gather_fusion.1 = bf16[32,64,512]{2,1,0:T(8,128)(2,1)} fusion(bf16[64,64,512]{2,1,0:T(8,128)(2,1)} %bitcast.9, s32[1024]{0:T(1024)S(1)} %pad_clamp_fusion), kind=kCustom, calls=%fused_computation.1.clone | custom fusion | bytes 4194432 | tf_op jit(solution)/shard_map/jit(_take)/gather | solution.py:39
  184.5 2.7 %broadcast_select_fusion.3 = (bf16[32,64,512]{2,1,0:T(8,128)(2,1)S(1)}, bf16[32,64,512]{2,1,0:T(8,128)(2,1)S(1)}) fusion(bf16[32,64,512]{2,1,0:T(8,128)(2,1)} %gather_fusion.1, pred[32]{0:T(512)(128)(4,1)S(1)} %get-tuple-element.6, bf16[32,64,512]{2,1,0:T(8,128)(2,1)} %gather_fusion.5), kind=kLoop, calls=%fused_computation.45 | loop fusion | flops 2097152 | bytes 8388640 | tf_op jit(solution)/shard_map/jit(_take)/select_n | solution.py:39
  187.2 1.8 fusion.97
  189.0 1.9 slice-done.1
  191.6 1.8 fusion.12
  193.4 2.1 copy-done.5
  195.5 1.2 exponential_reduce_fusion.3
  196.7 7.5 %fusion.31 = bf16[8,128,128]{1,2,0:T(8,128)(2,1)S(1)} fusion(f32[128,8]{0,1:T(8,128)S(1)} %exponential_reduce_fusion.3, bf16[2,8,512,128]{3,2,1,0:T(8,128)(2,1)} %param.22, bf16[128,512]{1,0:T(8,128)(2,1)S(1)} %copy-done.16, bf16[1024,512]{1,0:T(8,128)(2,1)} %bitcast.157, f32[128,8,1152]{2,0,1:T(8,128)} %copy-done.5), kind=kOutput, calls=%fused_computation.57 | convolution fusion | flops 1348733056 | bytes 11931648 | tf_op jit(solution)/shard_map/shc,hcv->shv/dot_general | solution.py:131
  204.3 4.9 %fusion.13 = f32[128,8,1152]{2,0,1:T(8,128)S(1)} fusion(f32[1152,128,8]{0,1,2:T(8,128)} %fusion.54, pred[128,1152]{1,0:T(8,128)(4,1)S(1)} %get-tuple-element.38, bf16[256,8,512]{0,2,1:T(8,128)(2,1)} %convert_bitcast_fusion.1, bf16[128,512]{1,0:T(8,128)(2,1)S(1)} %copy-done.15, bf16[1024,512]{1,0:T(8,128)(2,1)} %bitcast.154), kind=kOutput, calls=%fused_computation.29 | convolution fusion | flops 1213857792 | bytes 11812864 | tf_op jit(solution)/shard_map/shc,kc->shk/dot_general | solution.py:110
  209.3 2.2 copy-done.3
  211.5 1.1 exponential_reduce_fusion.2
  212.6 7.6 %fusion.30 = bf16[8,128,128]{1,2,0:T(8,128)(2,1)S(1)} fusion(f32[128,8]{0,1:T(8,128)S(1)} %exponential_reduce_fusion.2, bf16[2,8,512,128]{3,2,1,0:T(8,128)(2,1)} %param.22, bf16[128,512]{1,0:T(8,128)(2,1)S(1)} %copy-done.15, bf16[1024,512]{1,0:T(8,128)(2,1)} %bitcast.155, f32[128,8,1152]{2,0,1:T(8,128)} %copy-done.3), kind=kOutput, calls=%fused_computation.56 | convolution fusion | flops 1348733056 | bytes 11931648 | tf_op jit(solution)/shard_map/shc,hcv->shv/dot_general | solution.py:131
  220.4 4.4 %fusion.14 = f32[128,8,1152]{2,0,1:T(8,128)S(1)} fusion(f32[1152,128,8]{0,1,2:T(8,128)} %fusion.57, pred[128,1152]{1,0:T(8,128)(4,1)S(1)} %get-tuple-element.37, bf16[256,8,512]{0,2,1:T(8,128)(2,1)S(1)} %convert_bitcast_fusion, bf16[128,512]{1,0:T(8,128)(2,1)S(1)} %copy-done.14, bf16[1024,512]{1,0:T(8,128)(2,1)} %bitcast.152), kind=kOutput, calls=%fused_computation.30 | convolution fusion | flops 1213857792 | bytes 11812864 | tf_op jit(solution)/shard_map/shc,kc->shk/dot_general | solution.py:110
  224.8 2.2 copy-done.4
  227.0 1.1 exponential_reduce_fusion.1
  228.1 7.7 %fusion.29 = bf16[8,128,128]{1,2,0:T(8,128)(2,1)S(1)} fusion(f32[128,8]{0,1:T(8,128)S(1)} %exponential_reduce_fusion.1, bf16[2,8,512,128]{3,2,1,0:T(8,128)(2,1)} %param.22, bf16[128,512]{1,0:T(8,128)(2,1)S(1)} %copy-done.14, bf16[1024,512]{1,0:T(8,128)(2,1)} %bitcast.153, f32[128,8,1152]{2,0,1:T(8,128)} %copy-done.4), kind=kOutput, calls=%fused_computation.55 | convolution fusion | flops 1348733056 | bytes 11931648 | tf_op jit(solution)/shard_map/shc,hcv->shv/dot_general | solution.py:131
  236.6 4.5 %fusion.15 = f32[128,8,1152]{2,0,1:T(8,128)S(1)} fusion(f32[1152,128,8]{0,1,2:T(8,128)} %fusion.60, pred[128,1152]{1,0:T(8,128)(4,1)S(1)} %get-tuple-element.38, bf16[256,8,512]{0,2,1:T(8,128)(2,1)S(1)} %convert_bitcast_fusion, bf16[128,512]{1,0:T(8,128)(2,1)S(1)} %copy-done.13, bf16[1024,512]{1,0:T(8,128)(2,1)} %bitcast.150), kind=kOutput, calls=%fused_computation.31 | convolution fusion | flops 1213857792 | bytes 11812864 | tf_op jit(solution)/shard_map/shc,kc->shk/dot_general | solution.py:110
  241.1 2.1 copy-done.2
  243.2 1.3 exponential_reduce_fusion
  244.6 7.2 %fusion.28 = bf16[8,128,128]{1,2,0:T(8,128)(2,1)S(1)} fusion(f32[128,8]{0,1:T(8,128)S(1)} %exponential_reduce_fusion, bf16[2,8,512,128]{3,2,1,0:T(8,128)(2,1)} %param.22, bf16[128,512]{1,0:T(8,128)(2,1)S(1)} %copy-done.13, bf16[1024,512]{1,0:T(8,128)(2,1)S(1)} %bitcast.151, f32[128,8,1152]{2,0,1:T(8,128)} %copy-done.2), kind=kOutput, calls=%fused_computation.54 | convolution fusion | flops 1348733056 | bytes 11931648 | tf_op jit(solution)/shard_map/shc,hcv->shv/dot_general | solution.py:131
  252.0 1.1 pad_maximum_fusion
  (107 shorter events, 23.4 us)
Async XLA Ops:
  0.0 88.3 %copy-start = (s32[32,2]{0,1:T(2,128)S(1)}, s32[32,2]{0,1:T(2,128)}, u32[]{:S(2)}) copy-start(s32[32,2]{0,1:T(2,128)} %param.29) | copy-start | bytes 772
  1.6 2.5 %copy-start.22 = (s32[32,32]{1,0:T(8,128)}, s32[32,32]{1,0:T(8,128)S(1)}, u32[]{:S(2)}) copy-start(s32[32,32]{1,0:T(8,128)S(1)} %copy.149) | copy-start | bytes 12292
  3.2 0.6 copy-start.23
  8.2 17.7 %all-to-all-start.1 = ((bf16[32,2,4096]{2,1,0:T(2,128)(2,1)}), bf16[32,2,4096]{2,1,0:T(2,128)(2,1)S(1)}, u32[]{:S(2)}, u32[]{:S(2)}) async-start(bf16[32,2,4096]{2,1,0:T(2,128)(2,1)} %reshape.237), calls=%async_computation.1 | async-start | bytes 1048576 | tf_op jit(solution)/shard_map/all_to_all | solution.py:37
  25.9 11.7 %copy-start.10 = (bf16[32,2,4096]{2,1,0:T(2,128)(2,1)}, bf16[32,2,4096]{2,1,0:T(2,128)(2,1)S(1)}, u32[]{:S(2)}) copy-start(bf16[32,2,4096]{2,1,0:T(2,128)(2,1)S(1)} %all-to-all-done.1) | copy-start | bytes 1572868
  25.9 16.0 %all-to-all-start.3 = ((bf16[32,2,4096]{2,1,0:T(2,128)(2,1)}), bf16[32,2,4096]{2,1,0:T(2,128)(2,1)S(1)}, u32[]{:S(2)}, u32[]{:S(2)}) async-start(bf16[32,2,4096]{2,1,0:T(2,128)(2,1)} %reshape.243), calls=%async_computation.3 | async-start | bytes 1048576 | tf_op jit(solution)/shard_map/all_to_all | solution.py:37
  41.9 0.8 copy-start.11
  41.9 6.5 %copy-start.21 = (bf16[2,256,512]{2,1,0:T(8,128)(2,1)S(1)}, bf16[2,256,512]{2,1,0:T(8,128)(2,1)}, u32[]{:S(2)}) copy-start(bf16[2,256,512]{2,1,0:T(8,128)(2,1)} %param.20) | copy-start | bytes 1572868
  41.9 7.3 %copy-start.25 = (bf16[2,32,64]{2,1,0:T(8,128)(2,1)S(1)}, bf16[2,32,64]{2,1,0:T(8,128)(2,1)}, u32[]{:S(2)}) copy-start(bf16[2,32,64]{2,1,0:T(8,128)(2,1)} %param.24) | copy-start | bytes 24580
  42.7 75.6 %all-to-all-start.2 = ((bf16[32,2,64,512]{3,2,1,0:T(8,128)(2,1)}), bf16[32,2,64,512]{3,2,1,0:T(8,128)(2,1)}, u32[]{:S(2)}, u32[]{:S(2)}) async-start(bf16[32,2,64,512]{3,2,1,0:T(8,128)(2,1)} %bitcast.149), calls=%async_computation.2 | async-start | bytes 8388608 | tf_op jit(solution)/shard_map/all_to_all | solution.py:36
  48.4 67.8 %copy-start.9 = (bf16[2,8,128,512]{3,2,1,0:T(8,128)(2,1)S(1)}, bf16[2,8,128,512]{3,2,1,0:T(8,128)(2,1)}, u32[]{:S(2)}) copy-start(bf16[2,8,128,512]{3,2,1,0:T(8,128)(2,1)} %param.21) | copy-start | bytes 6291460
  118.3 62.0 %all-to-all-start = ((bf16[32,2,64,512]{3,2,1,0:T(8,128)(2,1)}), bf16[32,2,64,512]{3,2,1,0:T(8,128)(2,1)}, u32[]{:S(2)}, u32[]{:S(2)}) async-start(bf16[32,2,64,512]{3,2,1,0:T(8,128)(2,1)} %bitcast.148), calls=%async_computation | async-start | bytes 8388608 | tf_op jit(solution)/shard_map/all_to_all | solution.py:36
  130.8 3.7 %copy-start.24 = (bf16[1,128,64]{1,2,0:T(8,128)(2,1)S(1)}, bf16[1,128,64]{1,2,0:T(8,128)(2,1)}, u32[]{:S(2)}) copy-start(bf16[1,128,64]{1,2,0:T(8,128)(2,1)} %copy.197) | copy-start | bytes 49156
  132.9 1.6 copy-start.17
  132.9 4.6 %copy-start.18 = (bf16[1,128,512]{1,2,0:T(8,128)(2,1)S(1)}, bf16[1,128,512]{1,2,0:T(8,128)(2,1)}, u32[]{:S(2)}) copy-start(bf16[1,128,512]{1,2,0:T(8,128)(2,1)} %copy.165) | copy-start | bytes 393220
  134.5 6.0 %copy-start.19 = (bf16[1,128,512]{1,2,0:T(8,128)(2,1)S(1)}, bf16[1,128,512]{1,2,0:T(8,128)(2,1)}, u32[]{:S(2)}) copy-start(bf16[1,128,512]{1,2,0:T(8,128)(2,1)} %copy.175) | copy-start | bytes 393220
  137.5 6.1 %copy-start.20 = (bf16[1,128,512]{1,2,0:T(8,128)(2,1)S(1)}, bf16[1,128,512]{1,2,0:T(8,128)(2,1)}, u32[]{:S(2)}) copy-start(bf16[1,128,512]{1,2,0:T(8,128)(2,1)} %copy.181) | copy-start | bytes 393220
  184.5 4.6 %slice-start = ((s8[4718592]{0:T(1024)(128)(4,1)}), s8[524288]{0:T(1024)(128)(4,1)S(1)}, s32[]{:S(2)}) async-start(s8[4718592]{0:T(1024)(128)(4,1)} %bitcast.146), calls=%async_computation.4 | async-start | bytes 1048576
  187.2 3.7 %slice-start.1 = ((s8[4718592]{0:T(1024)(128)(4,1)}), s8[4194304]{0:T(1024)(128)(4,1)S(1)}, s32[]{:S(2)}) async-start(s8[4718592]{0:T(1024)(128)(4,1)} %bitcast.146), calls=%async_computation.5 | async-start | bytes 8388608
  187.2 4.4 %copy-start.6 = (bf16[256,8,512]{0,2,1:T(8,128)(2,1)S(1)}, bf16[256,8,512]{0,2,1:T(8,128)(2,1)}, u32[]{:S(2)}) copy-start(bf16[256,8,512]{0,2,1:T(8,128)(2,1)} %convert_bitcast_fusion.1) | copy-start | bytes 6291460
  187.2 4.4 %copy-start.16 = (bf16[128,512]{1,0:T(8,128)(2,1)S(1)}, bf16[128,512]{1,0:T(8,128)(2,1)}, u32[]{:S(2)}) copy-start(bf16[128,512]{1,0:T(8,128)(2,1)} %get-tuple-element.19) | copy-start | bytes 393220
  189.0 4.4 %copy-start.8 = (bf16[16,64,512]{2,1,0:T(8,128)(2,1)}, bf16[16,64,512]{2,1,0:T(8,128)(2,1)S(1)}, u32[]{:S(2)}) copy-start(bf16[16,64,512]{2,1,0:T(8,128)(2,1)S(1)} %get-tuple-element.10) | copy-start | bytes 3145732
  193.4 2.1 copy-start.5
  196.7 7.6 %copy-start.15 = (bf16[128,512]{1,0:T(8,128)(2,1)S(1)}, bf16[128,512]{1,0:T(8,128)(2,1)}, u32[]{:S(2)}) copy-start(bf16[128,512]{1,0:T(8,128)(2,1)} %get-tuple-element.22) | copy-start | bytes 393220
  209.3 2.2 copy-start.3
  212.6 7.8 %copy-start.14 = (bf16[128,512]{1,0:T(8,128)(2,1)S(1)}, bf16[128,512]{1,0:T(8,128)(2,1)}, u32[]{:S(2)}) copy-start(bf16[128,512]{1,0:T(8,128)(2,1)} %get-tuple-element.21) | copy-start | bytes 393220
  224.8 2.2 copy-start.4
  228.1 8.5 %copy-start.13 = (bf16[128,512]{1,0:T(8,128)(2,1)S(1)}, bf16[128,512]{1,0:T(8,128)(2,1)}, u32[]{:S(2)}) copy-start(bf16[128,512]{1,0:T(8,128)(2,1)} %get-tuple-element.20) | copy-start | bytes 393220
  241.1 2.1 copy-start.2
  243.2 1.3 copy-start.7
  244.6 7.4 %copy-start.12 = (bf16[128,1024]{1,0:T(8,128)(2,1)S(1)}, bf16[128,1024]{1,0:T(8,128)(2,1)}, u32[]{:S(2)}) copy-start(bf16[128,1024]{1,0:T(8,128)(2,1)} %copy.183) | copy-start | bytes 786436
  244.6 8.5 %copy-start.1 = (s32[32,2]{0,1:T(2,128)S(1)}, s32[32,2]{0,1:T(2,128)}, u32[]{:S(2)}) copy-start(s32[32,2]{0,1:T(2,128)} %param.29) | copy-start | bytes 772
where the time goes:
time: 254 us; the launch traced here: 253 us
  matrix products  61.5 us (24%)
  local copies, waits for them, and re-layouts  56.3 us (22%)
  blocking collectives  53.9 us (21%)
  waiting for transfers between devices  35.4 us (14%)
  starting transfers between devices  26.7 us (11%)
  other arithmetic  18.6 us (7%)
    dot_general x4, matrix products, per_device(): jnp.einsum('shc,hcv->shv', context, w_value[layer_index], preferred_eleme...  29.9 us
    all_to_all x2, waiting for transfers between devices, fetch_blocks(): lax.all_to_all(latent_out, 'group', split_axis=0, concat_axis=0, tiled=True)  29.6 us
    all_gather x1, blocking collectives, per_device(): lax.all_gather(suffix_rope, 'tp', axis=1, tiled=True)  28.2 us
    all_gather x1, blocking collectives, per_device(): lax.all_gather(suffix_latent, 'tp', axis=1, tiled=True)  25.7 us
    unnamed x63, local copies, waits for them, and re-layouts  17.6 us
    dot_general x4, matrix products, per_device(): jnp.einsum('shc,kc->shk', absorbed[first_row:first_row + suffix_len], key...  15.6 us
    all_to_all x2, starting transfers between devices, fetch_blocks(): lax.all_to_all(latent_out, 'group', split_axis=0, concat_axis=0, tiled=True)  13.4 us
    all_to_all x2, starting transfers between devices, fetch_blocks(): lax.all_to_all(rope_out, 'group', split_axis=0, concat_axis=0, tiled=True)  13.3 us
  transfers between devices with their start and end apart: 4, of which 3 were waited for; matrix products, arithmetic and copies ran while one was open for 22% of the time, Pallas kernels for 0%

commit v1 on v0

v1 whole, which is shorter than its diff:
```python
import functools
import math

import jax
import jax.numpy as jnp
from jax import lax
from jax.experimental import pallas as pl
from jax.experimental.pallas import tpu as pltpu
from jax.sharding import PartitionSpec as P

MESH = pl.DeviceIdType.MESH
BF16 = jnp.bfloat16
F32 = jnp.float32
CAP = 2
QUARTERS = 4


def dot(a, b):
    return jnp.dot(a, b, preferred_element_type=F32)


def dot_t(a, b):
    return lax.dot_general(a, b, (((1,), (1,)), ((), ())), preferred_element_type=F32)


def kernel(
    dims,
    ids,
    places,
    counts,
    qn_in,
    qr_in,
    wk_in,
    wv_in,
    sl_in,
    sr_in,
    pool_in,
    prope_in,
    out,
    qn,
    qr,
    wk,
    wv,
    pool0,
    pool1,
    prope,
    send0,
    send1,
    got0,
    got1,
    keys0,
    keys1,
    suf_lat,
    suf_rope,
    absorbed,
    qrope,
    in_sem,
    xy_send,
    xy_recv,
    suf_send,
    suf_recv,
    hop1_send,
    hop1_recv,
    hop2_send,
    hop2_recv,
):
    groups, tps, requests, blocks, suffix, heads, dc, dr, dn, dv = dims
    g_me = lax.axis_index("group")
    t_me = lax.axis_index("tp")
    right = lax.rem(t_me + 1, tps)
    left = lax.rem(t_me + tps - 1, tps)
    quarter = lax.rem(t_me, QUARTERS)
    q_left = lax.rem(quarter + QUARTERS - 1, QUARTERS)
    q_right = lax.rem(quarter + 1, QUARTERS)
    q_far = lax.rem(quarter + 2, QUARTERS)
    piece = 16
    seg = blocks * piece
    half = seg // 2
    rows = requests * suffix // tps
    pairs = heads // 2
    layers = 2
    scale = 1.0 / math.sqrt(dn + dr)

    first = pl.multiple_of(quarter * piece, piece)
    mine = pl.ds(pl.multiple_of(t_me * rows, rows), rows)
    loads = [
        pltpu.make_async_copy(pool_in.at[0, :, pl.ds(first, piece)], pool0, in_sem.at[0]),
        pltpu.make_async_copy(prope_in, prope, in_sem.at[1]),
        pltpu.make_async_copy(pool_in.at[1, :, pl.ds(first, piece)], pool1, in_sem.at[2]),
        pltpu.make_async_copy(sl_in, suf_lat.at[:, mine], in_sem.at[3]),
        pltpu.make_async_copy(sr_in, suf_rope.at[mine], in_sem.at[4]),
        pltpu.make_async_copy(qn_in, qn, in_sem.at[5]),
        pltpu.make_async_copy(wk_in, wk, in_sem.at[6]),
        pltpu.make_async_copy(qr_in, qr, in_sem.at[7]),
        pltpu.make_async_copy(wv_in, wv, in_sem.at[8]),
    ]
    for load in loads:
        load.start()

    barrier = pltpu.get_barrier_semaphore()

    def greet_group(i, carry):
        pl.semaphore_signal(
            barrier, inc=1, device_id={"group": lax.rem(g_me + i, groups)}, device_id_type=MESH
        )
        return carry

    def greet_tp(i, carry):
        pl.semaphore_signal(
            barrier, inc=1, device_id={"tp": lax.rem(t_me + i, tps)}, device_id_type=MESH
        )
        return carry

    lax.fori_loop(1, groups, greet_group, 0)
    lax.fori_loop(1, tps, greet_tp, 0)
    loads[0].wait()
    loads[1].wait()
    pl.semaphore_wait(barrier, groups + tps - 2)

    def plane_copy(layer, g):
        src, dst = ((send0, got0), (send1, got1))[layer]
        return pltpu.make_async_remote_copy(
            src_ref=src.at[g],
            dst_ref=dst.at[g_me],
            send_sem=xy_send.at[layer],
            recv_sem=xy_recv.at[layer],
            device_id={"group": g},
            device_id_type=MESH,
        )

    def fill0(i, carry):
        g = lax.rem(g_me + i, groups)
        for k in range(CAP):
            b = ids[g, k]
            send0[g, k, :, :dc] = pool0[b]
            send0[g, k, :, dc:] = prope[b]
        plane_copy(0, g).start()
        return carry

    lax.fori_loop(1, groups, fill0, 0)

    loads[3].wait()
    loads[4].wait()

    def suffix_copies(i):
        peer = lax.rem(t_me + i, tps)
        return [
            pltpu.make_async_remote_copy(
                src_ref=suf_lat.at[:, mine],
                dst_ref=suf_lat.at[:, mine],
                send_sem=suf_send.at[0],
                recv_sem=suf_recv.at[0],
                device_id={"tp": peer},
                device_id_type=MESH,
            ),
            pltpu.make_async_remote_copy(
                src_ref=suf_rope.at[mine],
                dst_ref=suf_rope.at[mine],
                send_sem=suf_send.at[1],
                recv_sem=suf_recv.at[1],
                device_id={"tp": peer},
                device_id_type=MESH,
            ),
        ]

    def send_suffix(i, carry):
        for copy in suffix_copies(i):
            copy.start()
        return carry

    lax.fori_loop(1, tps, send_suffix, 0)

    loads[2].wait()

    def fill1(i, carry):
        g = lax.rem(g_me + i, groups)
        for k in range(CAP):
            send1[g, k] = pool1[ids[g, k]]
        return carry

    lax.fori_loop(1, groups, fill1, 0)
    for k in range(CAP):
        got0[g_me, k] = jnp.zeros((piece, dc + 2 * dr), BF16)
        got1[g_me, k] = jnp.zeros((piece, dc), BF16)

    loads[5].wait()
    loads[6].wait()
    loads[7].wait()
    lane = lax.broadcasted_iota(jnp.int32, (suffix, 2 * dr), 1)

    def absorb(hp, carry):
        for layer in range(layers):
            for j in range(2):
                at = pl.ds(pl.multiple_of((hp * 2 + j) * dn, dn), dn)
                a = dot(qn[layer, :, at], wk[layer, hp * 2 + j]).astype(BF16)
                for r in range(requests):
                    absorbed[layer, r, hp, j * suffix : (j + 1) * suffix] = a[
                        r * suffix : (r + 1) * suffix
                    ]
            at = pl.ds(pl.multiple_of(hp * 2 * dr, 2 * dr), 2 * dr)
            for r in range(requests):
                both = qr[layer, r * suffix : (r + 1) * suffix, at].astype(F32)
                swapped = pltpu.roll(both, dr, 1)
                even, odd = (both, swapped) if layer == 0 else (swapped, both)
                live = (lane < dr) if layer == 0 else (lane >= dr)
                qrope[layer, r, hp, :suffix] = jnp.where(live, even, 0.0).astype(BF16)
                qrope[layer, r, hp, suffix:] = jnp.where(live, odd, 0.0).astype(BF16)
        return carry

    lax.fori_loop(0, pairs, absorb, 0)

    keys = (keys0, keys1)
    got = (got0, got1)

    def plane_wait(layer):
        pltpu.make_async_copy(
            got[layer].at[pl.ds(1, groups - 1)],
            got[layer].at[pl.ds(1, groups - 1)],
            xy_recv.at[layer],
        ).wait()

    def compact(layer):
        def one(b, carry):
            for r in range(requests):
                place = places[r * blocks + b]
                keys[layer][quarter, r, pl.ds(pl.multiple_of(b * piece, piece), piece)] = got[
                    layer
                ][place // CAP, place % CAP]
            return carry

        lax.fori_loop(0, blocks, one, 0)

    def ring_copy(ref, hop, unit, way):
        sems = ((hop1_send, hop1_recv), (hop2_send, hop2_recv))[hop]
        return pltpu.make_async_remote_copy(
            src_ref=ref,
            dst_ref=ref,
            send_sem=sems[0].at[unit, way],
            recv_sem=sems[1].at[unit, way],
            device_id={"tp": (right, left)[way]},
            device_id_type=MESH,
        )

    def hop1(layer, r, way):
        return ring_copy(keys[layer].at[quarter, r], 0, layer * requests + r, way)

    def hop1_in(layer, r, way):
        ref = keys[layer].at[(q_left, q_right)[way], r]
        return ring_copy(ref, 0, layer * requests + r, way)

    def hop2(layer, r, way):
        ref = keys[layer].at[(q_left, q_right)[way], r, pl.ds(way * half, half)]
        return ring_copy(ref, 1, layer * requests + r, way)

    def hop2_in(layer, r, way):
        ref = keys[layer].at[q_far, r, pl.ds(way * half, half)]
        return ring_copy(ref, 1, layer * requests + r, way)

    def forward(layer, r):
        for way in range(2):
            hop1_in(layer, r, way).wait_recv()
            hop2(layer, r, way).start()

    def arrived(layer, r):
        for way in range(2):
            hop2_in(layer, r, way).wait_recv()

    def send_ring(layer):
        for r in range(requests):
            for way in range(2):
                hop1(layer, r, way).start()

    def attend(layer, r):
        key_at = lax.broadcasted_iota(jnp.int32, (2 * suffix, seg), 1)
        live_prefix = key_at < counts[r] * piece
        query_at = lax.rem(lax.broadcasted_iota(jnp.int32, (2 * suffix, suffix), 0), suffix)
        live_suffix = lax.broadcasted_iota(jnp.int32, (2 * suffix, suffix), 1) <= query_at
        suffix_rows = slice(r * suffix, (r + 1) * suffix)

        def one(hp, carry):
            a = absorbed[layer, r, hp]
            qp = qrope[layer, r, hp]
            scores = []
            for q in range(QUARTERS):
                s = dot_t(a, keys[layer][q, r, :, :dc]) + dot_t(qp, keys0[q, r, :, dc:])
                scores.append(jnp.where(live_prefix, s * scale, -jnp.inf))
            s = dot_t(a, suf_lat[layer, suffix_rows]) + dot_t(qp, suf_rope[suffix_rows])
            last = jnp.where(live_suffix, s * scale, -jnp.inf)
            top = functools.reduce(jnp.maximum, scores).max(axis=1, keepdims=True)
            top = jnp.maximum(top, last.max(axis=1, keepdims=True))
            probs = [jnp.exp(s - top) for s in scores]
            last = jnp.exp(last - top)
            total = sum(probs).sum(axis=1, keepdims=True) + last.sum(axis=1, keepdims=True)
            context = dot(last.astype(BF16), suf_lat[layer, suffix_rows])
            for q in range(QUARTERS):
                context = context + dot(probs[q].astype(BF16), keys[layer][q, r, :, :dc])
            context = (context / total).astype(BF16)
            for j in range(2):
                h = hp * 2 + j
                out[layer, suffix_rows, pl.ds(pl.multiple_of(h * dv, dv), dv)] = dot(
                    context[j * suffix : (j + 1) * suffix], wv[layer, h]
                ).astype(BF16)
            return carry

        lax.fori_loop(0, pairs, one, 0)

    plane_wait(0)
    compact(0)

    def send1_step(i, carry):
        plane_copy(1, lax.rem(g_me + i, groups)).start()
        return carry

    send_ring(0)
    lax.fori_loop(1, groups, send1_step, 0)
    pltpu.make_async_copy(
        suf_lat.at[:, pl.ds(0, rows * (tps - 1))],
        suf_lat.at[:, pl.ds(0, rows * (tps - 1))],
        suf_recv.at[0],
    ).wait()
    pltpu.make_async_copy(
        suf_rope.at[pl.ds(0, rows * (tps - 1))],
        suf_rope.at[pl.ds(0, rows * (tps - 1))],
        suf_recv.at[1],
    ).wait()
    loads[8].wait()
    forward(0, 0)
    forward(0, 1)
    plane_wait(1)
    compact(1)
    send_ring(1)
    arrived(0, 0)
    attend(0, 0)
    forward(1, 0)
    arrived(0, 1)
    attend(0, 1)
    forward(1, 1)
    arrived(1, 0)
    attend(1, 0)
    arrived(1, 1)
    attend(1, 1)

    for layer in range(layers):
        pltpu.make_async_copy(
            (send0, send1)[layer].at[pl.ds(1, groups - 1)],
            (send0, send1)[layer].at[pl.ds(1, groups - 1)],
            xy_send.at[layer],
        ).wait()
        for r in range(requests):
            for way in range(2):
                hop1(layer, r, way).wait_send()
                hop2(layer, r, way).wait_send()
    pltpu.make_async_copy(
        suf_lat.at[:, pl.ds(0, rows * (tps - 1))],
        suf_lat.at[:, pl.ds(0, rows * (tps - 1))],
        suf_send.at[0],
    ).wait()
    pltpu.make_async_copy(
        suf_rope.at[pl.ds(0, rows * (tps - 1))],
        suf_rope.at[pl.ds(0, rows * (tps - 1))],
        suf_send.at[1],
    ).wait()


def slot_tables(block_holders, block_ids, groups, own_group):
    slots = block_holders.shape[1] * block_holders.shape[2]
    holders = block_holders.reshape(groups, slots)
    block_list = block_ids.reshape(groups, slots)
    order = jnp.arange(slots, dtype=jnp.int32)
    match = holders == own_group
    first = jnp.min(jnp.where(match, order, slots), axis=1, keepdims=True)
    final = jnp.max(jnp.where(match, order, -1), axis=1, keepdims=True)
    at = jnp.stack([order == first, order == final], axis=1)
    send_ids = jnp.sum(jnp.where(at, block_list[:, None, :], 0), axis=2)
    own = lax.dynamic_index_in_dim(holders, own_group, 0, keepdims=False)
    earlier = (own[None, :] == own[:, None]) & (order[None, :] < order[:, None])
    places = own * CAP + jnp.sum(earlier.astype(jnp.int32), axis=1)
    return send_ids, places


def per_device(
    queries_nope,
    queries_rope,
    w_key,
    w_value,
    suffix_latent,
    suffix_rope,
    pool_latent,
    pool_rope,
    block_holders,
    block_ids,
    prefix_blocks,
):
    groups = lax.axis_size("group")
    tps = lax.axis_size("tp")
    own_group = lax.axis_index("group")
    requests, blocks = block_holders.shape[1:]
    layers, tokens = queries_nope.shape[:2]
    suffix = tokens // requests
    heads, dn, dc = w_key.shape[1:]
    dv = w_value.shape[3]
    dr = suffix_rope.shape[2]
    held, length = pool_latent.shape[1:3]
    piece = length // QUARTERS
    seg = blocks * piece
    rows = suffix_latent.shape[1]
    ids, places = slot_tables(block_holders, block_ids, groups, own_group)
    counts = lax.dynamic_index_in_dim(prefix_blocks, own_group, 0, keepdims=False)
    quarter = lax.rem(lax.axis_index("tp"), QUARTERS)
    prope = lax.dynamic_slice_in_dim(pool_rope, quarter * piece * dr, piece * dr, 2)
    prope = prope.reshape(layers, held, piece, dr)
    prope = jnp.concatenate([prope[0], prope[1]], axis=-1)
    srope = jnp.concatenate([suffix_rope[0], suffix_rope[1]], axis=-1)
    dims = (groups, tps, requests, blocks, suffix, heads, dc, dr, dn, dv)
    smem = pl.BlockSpec(memory_space=pltpu.SMEM)
    hbm = pl.BlockSpec(memory_space=pl.ANY)
    units = layers * requests
    return pl.pallas_call(
        functools.partial(kernel, dims),
        out_shape=jax.ShapeDtypeStruct((layers, tokens, heads * dv), BF16),
        in_specs=[smem] * 3 + [hbm] * 8,
        out_specs=pl.BlockSpec(memory_space=pltpu.VMEM),
        scratch_shapes=[
            pltpu.VMEM(queries_nope.shape, BF16),
            pltpu.VMEM(queries_rope.shape, BF16),
            pltpu.VMEM(w_key.shape, BF16),
            pltpu.VMEM(w_value.shape, BF16),
            pltpu.VMEM((held, piece, dc), BF16),
            pltpu.VMEM((held, piece, dc), BF16),
            pltpu.VMEM((held, piece, 2 * dr), BF16),
            pltpu.VMEM((groups, CAP, piece, dc + 2 * dr), BF16),
            pltpu.VMEM((groups, CAP, piece, dc), BF16),
            pltpu.VMEM((groups, CAP, piece, dc + 2 * dr), BF16),
            pltpu.VMEM((groups, CAP, piece, dc), BF16),
            pltpu.VMEM((QUARTERS, requests, seg, dc + 2 * dr), BF16),
            pltpu.VMEM((QUARTERS, requests, seg, dc), BF16),
            pltpu.VMEM((layers, rows * tps, dc), BF16),
            pltpu.VMEM((rows * tps, 2 * dr), BF16),
            pltpu.VMEM((layers, requests, heads // 2, 2 * suffix, dc), BF16),
            pltpu.VMEM((layers, requests, heads // 2, 2 * suffix, 2 * dr), BF16),
            pltpu.SemaphoreType.DMA((9,)),
            pltpu.SemaphoreType.DMA((layers,)),
            pltpu.SemaphoreType.DMA((layers,)),
            pltpu.SemaphoreType.DMA((2,)),
            pltpu.SemaphoreType.DMA((2,)),
            pltpu.SemaphoreType.DMA((units, 2)),
            pltpu.SemaphoreType.DMA((units, 2)),
            pltpu.SemaphoreType.DMA((units, 2)),
            pltpu.SemaphoreType.DMA((units, 2)),
        ],
        compiler_params=pltpu.CompilerParams(
            collective_id=0, has_side_effects=True, vmem_limit_bytes=56 * 1024 * 1024
        ),
        cost_estimate=pl.CostEstimate(
            flops=12_000_000_000, bytes_accessed=12_000_000, transcendentals=5_000_000
        ),
    )(
        ids,
        places,
        counts,
        queries_nope,
        queries_rope,
        w_key,
        w_value,
        suffix_latent,
        srope,
        pool_latent,
        prope,
    )


def solution(mesh):
    in_specs = (
        P(None, "group", "tp"),
        P(None, "group", "tp"),
        P(None, "tp", None, None),
        P(None, "tp", None, None),
        P(None, ("group", "tp"), None),
        P(None, ("group", "tp"), None),
        P(None, "group", None, None),
        P(None, "group", None),
        P(),
        P(),
        P(),
    )
    out_specs = P(None, "group", "tp")
    return jax.shard_map(
        per_device, mesh=mesh, in_specs=in_specs, out_specs=out_specs, check_vma=False
    )
```

time: 254 us -> 96.2 us (0.38)
  the two profiles are of different devices: /device:TPU:8 before, /device:TPU:29 now
where the time goes in v1:
time: 96.2 us; the launch traced here: 95.7 us
  Pallas kernels  84.7 us (88%)
  local copies, waits for them, and re-layouts  7.78 us (8%)
  other arithmetic  3.14 us (3%)
    pallas_call x1, Pallas kernels, per_device(): pl.pallas_call(functools.partial(kernel, dims), out_shape=jax.ShapeDtypeS...  84.7 us
    unnamed x4, local copies, waits for them, and re-layouts  3.02 us

profile of v1, /device:TPU:29, one launch (start us, length us, event | category | flops | bytes accessed | tf_op | source)
XLA Modules:
  0.0 95.7 jit_solution(6009989949463211513)
XLA Ops:
  0.0 0.0 copy-start
  0.0 0.7 copy-done
  0.7 0.8 dynamic-slice_reduce_fusion.counts
  1.4 0.8 select_reduce_fusion.2
  2.3 0.1 iota_compare_fusion.1
  2.3 0.8 constant_dynamic-slice_fusion.2
  3.1 0.1 copy.17
  3.2 0.2 convert_reduce_fusion
  3.4 0.6 multiply_add_fusion.1.places
  3.9 0.8 copy.14
  4.7 0.1 select_reduce_fusion
  4.8 0.7 copy.16.ids
  5.5 0.7 slice_bitcast_fusion.1
  6.3 0.7 pad_maximum_fusion.1.sr_in
  6.9 0.8 constant_dynamic-slice_fusion.1
  7.7 0.1 squeeze.24
  7.8 0.1 squeeze.25
  7.9 0.7 pad_maximum_fusion.prope_in
  8.7 84.7 %shard_map.109 = bf16[2,256,1024]{2,1,0:T(8,128)(2,1)} custom-call(s32[32,2]{1,0:T(8,128)} %copy.16.ids, s32[32]{0:T(128)} %multiply_add_fusion.1.places, s32[2]{0:T(128)} %dynamic-slice_reduce_fusion.counts, bf16[2,256,1024]{2,1,0:T(8,128)(2,1)} %qn_in.1, bf16[2,256,512]{2,1,0:T(8,128)(2,1)} %qr_in.1, bf16[2,8,128,512]{3,2,1,0:T(8,128)(2,1)} %wk_in.1, ...), custom_call_target="tpu_custom_call" | custom-call | flops 12000000000 | bytes 12000000 | tf_op jit(solution)/shard_map/pallas_call | solution.py:418
  93.4 2.3 %copy.19 = bf16[2,256,1024]{2,1,0:T(8,128)(2,1)} copy(bf16[2,256,1024]{2,1,0:T(8,128)(2,1)} %shard_map.109) | data formatting | bytes 2097152
  (1 shorter events, 0.0 us)
Async XLA Ops:
  0.0 0.7 copy-start

commit v2 on v1

v2 whole, which is shorter than its diff:
```python
import functools
import math

import jax
import jax.numpy as jnp
from jax import lax
from jax.experimental import pallas as pl
from jax.experimental.pallas import tpu as pltpu
from jax.sharding import PartitionSpec as P

MESH = pl.DeviceIdType.MESH
BF16 = jnp.bfloat16
F32 = jnp.float32
CAP = 2
QUARTERS = 4


def dot(a, b):
    return jnp.dot(a, b, preferred_element_type=F32)


def dot_t(a, b):
    return lax.dot_general(a, b, (((1,), (1,)), ((), ())), preferred_element_type=F32)


def torus_peer(g_me, groups, i):
    if groups != 32:
        return lax.rem(g_me + i, groups)
    x, y, c = g_me // 8, lax.rem(g_me // 2, 4), lax.rem(g_me, 2)
    x = lax.rem(x + i, 4)
    y = lax.rem(y + i + i // 4, 4)
    c = lax.rem(c + i // 16, 2)
    return x * 8 + y * 2 + c


def kernel(
    dims,
    holders,
    block_ids,
    prefix_blocks,
    qn_in,
    qr_in,
    wk_in,
    wv_in,
    sl_in,
    sr_in,
    pool_in,
    prope_in,
    out,
    qn,
    qr,
    wk,
    wv,
    pools,
    prope_lanes,
    prope_wide,
    prope,
    srope,
    sends,
    gots,
    keys,
    sufs,
    absorbed,
    qrope,
    picks,
    ranks,
    in_sem,
    xy_send,
    xy_recv,
    suf_send,
    suf_recv,
    hop1_send,
    hop1_recv,
    hop2_send,
    hop2_recv,
):
    groups, tps, requests, blocks, suffix, heads, dc, dr, dn, dv = dims
    g_me = lax.axis_index("group")
    t_me = lax.axis_index("tp")
    right = lax.rem(t_me + 1, tps)
    left = lax.rem(t_me + tps - 1, tps)
    quarter = lax.rem(t_me, QUARTERS)
    q_left = lax.rem(quarter + QUARTERS - 1, QUARTERS)
    q_right = lax.rem(quarter + 1, QUARTERS)
    q_far = lax.rem(quarter + 2, QUARTERS)
    piece = 16
    seg = blocks * piece
    half = seg // 2
    rows = requests * suffix // tps
    pairs = heads // 2
    layers = 2
    hw = dc // 2
    scale = math.log2(math.e) / math.sqrt(dn + dr)

    first = pl.multiple_of(quarter * piece, piece)
    lanes = pl.ds(pl.multiple_of(quarter * piece * dr, piece * dr), piece * dr)
    tokens = pl.ds(first, piece)
    mine = pl.ds(pl.multiple_of(t_me * rows, rows), rows)
    loads = [
        pltpu.make_async_copy(pool_in.at[0, :, tokens, pl.ds(0, hw)], pools[0], in_sem.at[0]),
        pltpu.make_async_copy(sl_in.at[0], sufs[0].at[mine, pl.ds(0, dc)], in_sem.at[1]),
        pltpu.make_async_copy(sl_in.at[1], sufs[1].at[mine], in_sem.at[2]),
        pltpu.make_async_copy(sr_in, srope, in_sem.at[3]),
        pltpu.make_async_copy(pool_in.at[0, :, tokens, pl.ds(hw, hw)], pools[1], in_sem.at[4]),
        pltpu.make_async_copy(prope_in.at[:, :, lanes], prope_lanes, in_sem.at[5]),
        pltpu.make_async_copy(pool_in.at[1, :, tokens, pl.ds(0, hw)], pools[2], in_sem.at[6]),
        pltpu.make_async_copy(pool_in.at[1, :, tokens, pl.ds(hw, hw)], pools[3], in_sem.at[7]),
        pltpu.make_async_copy(qn_in, qn, in_sem.at[8]),
        pltpu.make_async_copy(wk_in, wk, in_sem.at[9]),
        pltpu.make_async_copy(qr_in, qr, in_sem.at[10]),
        pltpu.make_async_copy(wv_in, wv, in_sem.at[11]),
    ]
    for load in loads:
        load.start()

    barrier = pltpu.get_barrier_semaphore()

    def greet(i, carry):
        pl.semaphore_signal(
            barrier, inc=1, device_id={"group": torus_peer(g_me, groups, i)}, device_id_type=MESH
        )
        return carry

    for neighbour in (left, right):
        pl.semaphore_signal(barrier, inc=1, device_id={"tp": neighbour}, device_id_type=MESH)
    lax.fori_loop(1, groups, greet, 0)

    slots = [(r, j) for r in range(requests) for j in range(blocks)]

    def table(i, carry):
        g = torus_peer(g_me, groups, i)
        listed = [holders[g, r, j] == g_me for r, j in slots]
        names = [block_ids[g, r, j] for r, j in slots]
        final = jnp.int32(0)
        for m, b in zip(listed, names):
            final = jnp.where(m, b, final)
        early = jnp.int32(0)
        for m, b in zip(listed[::-1], names[::-1]):
            early = jnp.where(m, b, early)
        picks[g, 0] = early
        picks[g, 1] = final
        return carry

    def fill(c):
        def one(i, carry):
            g = torus_peer(g_me, groups, i)
            for k in range(CAP):
                b = picks[g, k]
                if c == 1:
                    sends[c][g, k, :, :hw] = pools[c][b]
                    sends[c][g, k, :, hw:] = prope[b]
                else:
                    sends[c][g, k] = pools[c][b]
            return carry

        lax.fori_loop(1, groups, one, 0)

    def plane_copy(c, g):
        return pltpu.make_async_remote_copy(
            src_ref=sends[c].at[g],
            dst_ref=gots[c].at[g_me],
            send_sem=xy_send.at[c],
            recv_sem=xy_recv.at[c],
            device_id={"group": g},
            device_id_type=MESH,
        )

    def plane_send(c):
        def one(i, carry):
            plane_copy(c, torus_peer(g_me, groups, i)).start()
            return carry

        lax.fori_loop(1, groups, one, 0)

    def others(ref):
        return ref.at[pl.ds(1, groups - 1)]

    def plane_wait(c):
        pltpu.make_async_copy(others(gots[c]), others(gots[c]), xy_recv.at[c]).wait()

    def suffix_copy(h, way, layer, arriving):
        step = h + 1 if arriving else h
        origin = lax.rem(t_me + (tps - step if way == 0 else step), tps)
        ref = sufs[layer].at[pl.ds(pl.multiple_of(origin * rows, rows), rows)]
        return pltpu.make_async_remote_copy(
            src_ref=ref,
            dst_ref=ref,
            send_sem=suf_send.at[h, way, layer],
            recv_sem=suf_recv.at[h, way, layer],
            device_id={"tp": (right, left)[way]},
            device_id_type=MESH,
        )

    last_hop = tps // 2 - 1

    def carried(h, way):
        return (0, 1) if h < last_hop else (way,)

    def suffix_send(h):
        for way in range(2):
            for layer in carried(h, way):
                suffix_copy(h, way, layer, False).start()

    def suffix_wait(h):
        for way in range(2):
            for layer in carried(h, way):
                suffix_copy(h, way, layer, True).wait_recv()

    def suffix_forward(h):
        suffix_wait(h - 1)
        suffix_send(h)

    lax.fori_loop(1, groups, table, 0)
    loads[0].wait()
    fill(0)
    for at in (1, 2, 3):
        loads[at].wait()
    sufs[0][mine, dc:] = jnp.concatenate(
        [srope[0].astype(F32), srope[1].astype(F32)], axis=1
    ).astype(BF16)
    pl.semaphore_wait(barrier, groups + 1)
    plane_send(0)
    suffix_send(0)

    loads[4].wait()
    loads[5].wait()
    held = prope.shape[0]
    low = lax.broadcasted_iota(jnp.int32, (held, 2 * dr), 1) < dr
    for j in range(piece // 2):
        x0 = prope_lanes[0, :, 2 * dr * j : 2 * dr * (j + 1)].astype(F32)
        x1 = prope_lanes[1, :, 2 * dr * j : 2 * dr * (j + 1)].astype(F32)
        prope_wide[:, 2 * j, :] = jnp.where(low, x0, pltpu.roll(x1, dr, 1))
        prope_wide[:, 2 * j + 1, :] = jnp.where(low, pltpu.roll(x0, dr, 1), x1)
    prope[...] = prope_wide[...].astype(BF16)
    fill(1)
    plane_send(1)

    own = [holders[g_me, r, j] for r, j in slots]
    for s, (r, j) in enumerate(slots):
        rank = jnp.int32(0)
        for h in own[:s]:
            rank = jnp.where(h == own[s], 1, rank)
        ranks[r, j] = rank
    for c in range(4):
        for k in range(CAP):
            gots[c][g_me, k] = jnp.zeros(gots[c].shape[2:], BF16)

    lane = lax.broadcasted_iota(jnp.int32, (suffix, 2 * dr), 1)

    def absorb(layer):
        def one(hp, carry):
            for j in range(2):
                at = pl.ds(pl.multiple_of((hp * 2 + j) * dn, dn), dn)
                a = dot(qn[layer, :, at], wk[layer, hp * 2 + j]).astype(BF16)
                for r in range(requests):
                    absorbed[layer, r, hp, j * suffix : (j + 1) * suffix] = a[
                        r * suffix : (r + 1) * suffix
                    ]
            at = pl.ds(pl.multiple_of(hp * 2 * dr, 2 * dr), 2 * dr)
            for r in range(requests):
                both = qr[layer, r * suffix : (r + 1) * suffix, at].astype(F32)
                swapped = pltpu.roll(both, dr, 1)
                even, odd = (both, swapped) if layer == 0 else (swapped, both)
                live = (lane < dr) if layer == 0 else (lane >= dr)
                qrope[layer, r, hp, :suffix] = jnp.where(live, even, 0.0).astype(BF16)
                qrope[layer, r, hp, suffix:] = jnp.where(live, odd, 0.0).astype(BF16)
            return carry

        lax.fori_loop(0, pairs, one, 0)

    def compact(c):
        def one(b, carry):
            for r in range(requests):
                at = pl.ds(pl.multiple_of(b * piece, piece), piece)
                keys[c][quarter, r, at] = gots[c][holders[g_me, r, b], ranks[r, b]]
            return carry

        lax.fori_loop(0, blocks, one, 0)

    def ring_copy(ref, hop, unit, way):
        sems = ((hop1_send, hop1_recv), (hop2_send, hop2_recv))[hop]
        return pltpu.make_async_remote_copy(
            src_ref=ref,
            dst_ref=ref,
            send_sem=sems[0].at[unit, way],
            recv_sem=sems[1].at[unit, way],
            device_id={"tp": (right, left)[way]},
            device_id_type=MESH,
        )

    def hop1(c, r, way):
        return ring_copy(keys[c].at[quarter, r], 0, c * requests + r, way)

    def hop1_in(c, r, way):
        return ring_copy(keys[c].at[(q_left, q_right)[way], r], 0, c * requests + r, way)

    def hop2(c, r, way):
        ref = keys[c].at[(q_left, q_right)[way], r, pl.ds(way * half, half)]
        return ring_copy(ref, 1, c * requests + r, way)

    def hop2_in(c, r, way):
        ref = keys[c].at[q_far, r, pl.ds(way * half, half)]
        return ring_copy(ref, 1, c * requests + r, way)

    def ring_send(c, r):
        for way in range(2):
            hop1(c, r, way).start()

    def forward(c, r):
        for way in range(2):
            hop1_in(c, r, way).wait_recv()
            hop2(c, r, way).start()

    def arrived(c, r):
        for way in range(2):
            hop2_in(c, r, way).wait_recv()

    def attend(layer, r, begin, end):
        ka, kb = keys[2 * layer], keys[2 * layer + 1]
        key_at = lax.broadcasted_iota(jnp.int32, (2 * suffix, seg), 1)
        live_prefix = key_at < prefix_blocks[g_me, r] * piece
        query_at = lax.rem(lax.broadcasted_iota(jnp.int32, (2 * suffix, suffix), 0), suffix)
        live_suffix = lax.broadcasted_iota(jnp.int32, (2 * suffix, suffix), 1) <= query_at
        suffix_rows = slice(r * suffix, (r + 1) * suffix)

        def one(hp, carry):
            a = absorbed[layer, r, hp]
            qp = qrope[layer, r, hp]
            scores = []
            for q in range(QUARTERS):
                s = dot_t(a[:, :hw], ka[q, r]) + dot_t(a[:, hw:], kb[q, r, :, :hw])
                s = s + dot_t(qp, keys[1][q, r, :, hw:])
                scores.append(jnp.where(live_prefix, s, -jnp.inf))
            s = dot_t(a, sufs[layer][suffix_rows, :dc]) + dot_t(qp, sufs[0][suffix_rows, dc:])
            last = jnp.where(live_suffix, s, -jnp.inf)
            top = functools.reduce(jnp.maximum, scores).max(axis=1, keepdims=True)
            top = jnp.maximum(top, last.max(axis=1, keepdims=True)) * scale
            probs = [jnp.exp2(s * scale - top) for s in scores]
            last = jnp.exp2(last * scale - top)
            total = sum(probs).sum(axis=1, keepdims=True) + last.sum(axis=1, keepdims=True)
            probs = [p.astype(BF16) for p in probs]
            last = last.astype(BF16)
            halves = []
            for side in range(2):
                context = dot(last, sufs[layer][suffix_rows, side * hw : (side + 1) * hw])
                for q in range(QUARTERS):
                    context = context + dot(probs[q], (ka, kb)[side][q, r, :, :hw])
                halves.append(context)
            inverse = 1.0 / total
            context = jnp.concatenate([(h * inverse).astype(BF16) for h in halves], axis=1)
            for j in range(2):
                h = hp * 2 + j
                out[layer, suffix_rows, pl.ds(pl.multiple_of(h * dv, dv), dv)] = dot(
                    context[j * suffix : (j + 1) * suffix], wv[layer, h]
                ).astype(BF16)
            return carry

        lax.fori_loop(begin, end, one, 0)

    mid = pairs // 2
    for at in (8, 9, 10):
        loads[at].wait()
    if last_hop > 1:
        suffix_forward(1)
    absorb(0)
    if last_hop > 2:
        suffix_forward(2)
    loads[6].wait()
    loads[7].wait()
    fill(2)
    fill(3)
    plane_wait(0)
    compact(0)
    ring_send(0, 0)
    ring_send(0, 1)
    plane_send(2)
    suffix_forward(last_hop)
    absorb(1)
    plane_wait(1)
    compact(1)
    ring_send(1, 0)
    ring_send(1, 1)
    plane_send(3)
    forward(0, 0)
    forward(0, 1)
    suffix_wait(last_hop)
    loads[11].wait()
    forward(1, 0)
    plane_wait(2)
    compact(2)
    ring_send(2, 0)
    forward(1, 1)
    plane_wait(3)
    compact(3)
    ring_send(3, 0)
    ring_send(2, 1)
    ring_send(3, 1)
    arrived(0, 0)
    arrived(1, 0)
    attend(0, 0, 0, mid)
    forward(2, 0)
    attend(0, 0, mid, pairs)
    forward(3, 0)
    arrived(0, 1)
    arrived(1, 1)
    attend(0, 1, 0, mid)
    forward(2, 1)
    attend(0, 1, mid, pairs)
    forward(3, 1)
    arrived(2, 0)
    arrived(3, 0)
    attend(1, 0, 0, pairs)
    arrived(2, 1)
    arrived(3, 1)
    attend(1, 1, 0, pairs)

    for c in range(4):
        pltpu.make_async_copy(others(sends[c]), others(sends[c]), xy_send.at[c]).wait()
        for r in range(requests):
            for way in range(2):
                hop1(c, r, way).wait_send()
                hop2(c, r, way).wait_send()
    for h in range(last_hop + 1):
        for way in range(2):
            for layer in carried(h, way):
                suffix_copy(h, way, layer, False).wait_send()


def per_device(
    queries_nope,
    queries_rope,
    w_key,
    w_value,
    suffix_latent,
    suffix_rope,
    pool_latent,
    pool_rope,
    block_holders,
    block_ids,
    prefix_blocks,
):
    groups = lax.axis_size("group")
    tps = lax.axis_size("tp")
    requests, blocks = block_holders.shape[1:]
    layers, tokens = queries_nope.shape[:2]
    suffix = tokens // requests
    heads, dn, dc = w_key.shape[1:]
    dv = w_value.shape[3]
    dr = suffix_rope.shape[2]
    held, length = pool_latent.shape[1:3]
    piece = length // QUARTERS
    seg = blocks * piece
    rows = suffix_latent.shape[1]
    dims = (groups, tps, requests, blocks, suffix, heads, dc, dr, dn, dv)
    smem = pl.BlockSpec(memory_space=pltpu.SMEM)
    hbm = pl.BlockSpec(memory_space=pl.ANY)
    hw = dc // 2
    widths = (hw, hw + 2 * dr, hw, hw)
    units = 4 * requests
    landing = [pltpu.VMEM((groups, CAP, piece, w), BF16) for w in widths]
    hops = tps // 2
    return pl.pallas_call(
        functools.partial(kernel, dims),
        out_shape=jax.ShapeDtypeStruct((layers, tokens, heads * dv), BF16),
        in_specs=[smem] * 3 + [hbm] * 8,
        out_specs=pl.BlockSpec(memory_space=pltpu.VMEM),
        scratch_shapes=[
            pltpu.VMEM(queries_nope.shape, BF16),
            pltpu.VMEM(queries_rope.shape, BF16),
            pltpu.VMEM(w_key.shape, BF16),
            pltpu.VMEM(w_value.shape, BF16),
            [pltpu.VMEM((held, piece, hw), BF16) for _ in range(4)],
            pltpu.VMEM((layers, held, piece * dr), BF16),
            pltpu.VMEM((held, piece, 2 * dr), F32),
            pltpu.VMEM((held, piece, 2 * dr), BF16),
            pltpu.VMEM((layers, rows, dr), BF16),
            landing,
            landing,
            [pltpu.VMEM((QUARTERS, requests, seg, w), BF16) for w in widths],
            [pltpu.VMEM((rows * tps, w), BF16) for w in (dc + 2 * dr, dc)],
            pltpu.VMEM((layers, requests, heads // 2, 2 * suffix, dc), BF16),
            pltpu.VMEM((layers, requests, heads // 2, 2 * suffix, 2 * dr), BF16),
            pltpu.SMEM((groups, CAP), jnp.int32),
            pltpu.SMEM((requests, blocks), jnp.int32),
            pltpu.SemaphoreType.DMA((12,)),
            pltpu.SemaphoreType.DMA((4,)),
            pltpu.SemaphoreType.DMA((4,)),
            pltpu.SemaphoreType.DMA((hops, 2, 2)),
            pltpu.SemaphoreType.DMA((hops, 2, 2)),
            pltpu.SemaphoreType.DMA((units, 2)),
            pltpu.SemaphoreType.DMA((units, 2)),
            pltpu.SemaphoreType.DMA((units, 2)),
            pltpu.SemaphoreType.DMA((units, 2)),
        ],
        compiler_params=pltpu.CompilerParams(
            collective_id=0, has_side_effects=True, vmem_limit_bytes=56 * 1024 * 1024
        ),
        cost_estimate=pl.CostEstimate(
            flops=12_000_000_000, bytes_accessed=12_000_000, transcendentals=5_000_000
        ),
    )(
        block_holders,
        block_ids,
        prefix_blocks,
        queries_nope,
        queries_rope,
        w_key,
        w_value,
        suffix_latent,
        suffix_rope,
        pool_latent,
        pool_rope,
    )


def solution(mesh):
    in_specs = (
        P(None, "group", "tp"),
        P(None, "group", "tp"),
        P(None, "tp", None, None),
        P(None, "tp", None, None),
        P(None, ("group", "tp"), None),
        P(None, ("group", "tp"), None),
        P(None, "group", None, None),
        P(None, "group", None),
        P(),
        P(),
        P(),
    )
    out_specs = P(None, "group", "tp")
    return jax.shard_map(
        per_device, mesh=mesh, in_specs=in_specs, out_specs=out_specs, check_vma=False
    )
```

time: 96.2 us -> 86.9 us (0.903)
  the two profiles are of different devices: /device:TPU:29 before, /device:TPU:1 now
where the time goes in v2:
time: 86.9 us; the launch traced here: 86.5 us
  Pallas kernels  80.1 us (92%)
  local copies, waits for them, and re-layouts  6.41 us (7%)
    pallas_call x1, Pallas kernels, per_device(): pl.pallas_call(functools.partial(kernel, dims), out_shape=jax.ShapeDtypeS...  80.1 us
    unnamed x4, local copies, waits for them, and re-layouts  6.41 us

profile of v2, /device:TPU:1, one launch (start us, length us, event | category | flops | bytes accessed | tf_op | source)
XLA Modules:
  0.0 86.5 jit_solution(5406541341394509914)
XLA Ops:
  0.0 1.4 %copy.14.prefix_blocks = s32[32,2]{1,0:T(8,128)} copy(s32[32,2]{0,1:T(2,128)} %param.21) | data formatting | bytes 512 | tf_op args[10]
  1.4 1.4 %copy.12.holders = s32[32,2,16]{2,1,0:T(2,128)} copy(s32[32,2,16]{0,2,1:T(8,128)} %param.19) | data formatting | bytes 8192 | tf_op args[8]
  2.8 1.4 %copy.13.block_ids = s32[32,2,16]{2,1,0:T(2,128)} copy(s32[32,2,16]{0,2,1:T(8,128)} %param.20) | data formatting | bytes 8192 | tf_op args[9]
  4.2 80.1 %shard_map.109 = bf16[2,256,1024]{2,1,0:T(8,128)(2,1)} custom-call(s32[32,2,16]{2,1,0:T(2,128)} %copy.12.holders, s32[32,2,16]{2,1,0:T(2,128)} %copy.13.block_ids, s32[32,2]{1,0:T(8,128)} %copy.14.prefix_blocks, bf16[2,256,1024]{2,1,0:T(8,128)(2,1)} %qn_in.1, bf16[2,256,512]{2,1,0:T(8,128)(2,1)} %qr_in.1, bf16[2,8,128,512]{3,2,1,0:T(8,128)(2,1)} %wk_in.1, ...), custom_call_target="tpu_custom_call" | custom-call | flops 12000000000 | bytes 12000000 | tf_op jit(solution)/shard_map/pallas_call | solution.py:462
  84.3 2.3 %copy.16 = bf16[2,256,1024]{2,1,0:T(8,128)(2,1)} copy(bf16[2,256,1024]{2,1,0:T(8,128)(2,1)} %shard_map.109) | data formatting | bytes 2097152

commit v3 on v2

v3 whole, which is shorter than its diff:
```python
import functools
import math

import jax
import jax.numpy as jnp
from jax import lax
from jax.experimental import pallas as pl
from jax.experimental.pallas import tpu as pltpu
from jax.sharding import PartitionSpec as P

MESH = pl.DeviceIdType.MESH
BF16 = jnp.bfloat16
F32 = jnp.float32
CAP = 2
QUARTERS = 4


def dot(a, b):
    return jnp.dot(a, b, preferred_element_type=F32)


def dot_t(a, b):
    return lax.dot_general(a, b, (((1,), (1,)), ((), ())), preferred_element_type=F32)


def torus_peer(g_me, groups, i):
    if groups != 32:
        return lax.rem(g_me + i, groups)
    x, y, c = g_me // 8, lax.rem(g_me // 2, 4), lax.rem(g_me, 2)
    x = lax.rem(x + i, 4)
    y = lax.rem(y + i + i // 4, 4)
    c = lax.rem(c + i // 16, 2)
    return x * 8 + y * 2 + c


def kernel(
    dims,
    holders,
    block_ids,
    prefix_blocks,
    qn_in,
    qr_in,
    wk_in,
    wv_in,
    sl_in,
    sr_in,
    pool_in,
    prope_in,
    out,
    qn,
    qr,
    wk,
    wv,
    pools,
    prope_lanes,
    prope_wide,
    prope,
    srope,
    sends,
    gots,
    keys,
    sufs,
    absorbed0,
    absorbed1,
    held_top,
    held_total,
    held_context,
    picks,
    ranks,
    in_sem,
    xy_send,
    xy_recv,
    suf_send,
    suf_recv,
    hop1_send,
    hop1_recv,
    hop2_send,
    hop2_recv,
):
    groups, tps, requests, blocks, suffix, heads, dc, dr, dn, dv = dims
    g_me = lax.axis_index("group")
    t_me = lax.axis_index("tp")
    right = lax.rem(t_me + 1, tps)
    left = lax.rem(t_me + tps - 1, tps)
    quarter = lax.rem(t_me, QUARTERS)
    q_left = lax.rem(quarter + QUARTERS - 1, QUARTERS)
    q_right = lax.rem(quarter + 1, QUARTERS)
    q_far = lax.rem(quarter + 2, QUARTERS)
    piece = 16
    widths = (dc // 4, dc // 4 + 2 * dr, dc // 2, dc // 2, dc // 2)
    places = (0, dc // 4, dc // 2 + 2 * dr, 0, dc // 2)
    whole = pl.ds(0, blocks * piece)
    seg = blocks * piece
    half = seg // 2
    rows = requests * suffix // tps
    pairs = heads // 2
    layers = 2
    hw = dc // 2
    qw = dc // 4
    rw = 2 * dr
    final = 4
    scale = math.log2(math.e) / math.sqrt(dn + dr)

    first = pl.multiple_of(quarter * piece, piece)
    lanes = pl.ds(pl.multiple_of(quarter * piece * dr, piece * dr), piece * dr)
    tokens = pl.ds(first, piece)
    far = pl.ds(pl.multiple_of(q_far * piece, piece), piece)
    mine = pl.ds(pl.multiple_of(t_me * rows, rows), rows)
    loads = [
        pltpu.make_async_copy(pool_in.at[0, :, tokens, pl.ds(0, qw)], pools[0], in_sem.at[0]),
        pltpu.make_async_copy(sl_in.at[0, :, pl.ds(0, hw)], sufs[0].at[mine, pl.ds(0, hw)], in_sem.at[1]),
        pltpu.make_async_copy(
            sl_in.at[0, :, pl.ds(hw, hw)], sufs[0].at[mine, pl.ds(hw + rw, hw)], in_sem.at[2]
        ),
        pltpu.make_async_copy(sl_in.at[1], sufs[1].at[mine, pl.ds(0, dc)], in_sem.at[3]),
        pltpu.make_async_copy(sr_in, srope, in_sem.at[4]),
        pltpu.make_async_copy(pool_in.at[0, :, tokens, pl.ds(qw, qw)], pools[1], in_sem.at[5]),
        pltpu.make_async_copy(prope_in.at[:, :, lanes], prope_lanes, in_sem.at[6]),
        pltpu.make_async_copy(pool_in.at[0, :, tokens, pl.ds(hw, hw)], pools[2], in_sem.at[7]),
        pltpu.make_async_copy(pool_in.at[1, :, tokens, pl.ds(0, hw)], pools[3], in_sem.at[8]),
        pltpu.make_async_copy(qn_in, qn, in_sem.at[9]),
        pltpu.make_async_copy(wk_in, wk, in_sem.at[10]),
        pltpu.make_async_copy(qr_in, qr, in_sem.at[11]),
        pltpu.make_async_copy(pool_in.at[1, :, tokens, pl.ds(hw, hw)], pools[4], in_sem.at[12]),
        pltpu.make_async_copy(pool_in.at[1, :, far, pl.ds(hw, hw)], pools[5], in_sem.at[13]),
        pltpu.make_async_copy(wv_in, wv, in_sem.at[14]),
    ]
    for load in loads:
        load.start()

    barrier = pltpu.get_barrier_semaphore()

    def greet(i, carry):
        pl.semaphore_signal(
            barrier, inc=1, device_id={"group": torus_peer(g_me, groups, i)}, device_id_type=MESH
        )
        return carry

    for neighbour in (left, right):
        pl.semaphore_signal(barrier, inc=1, device_id={"tp": neighbour}, device_id_type=MESH)
    lax.fori_loop(1, groups, greet, 0)

    slots = [(r, j) for r in range(requests) for j in range(blocks)]

    def table(g):
        names = [block_ids[r, j, g] for r, j in slots]
        own = [holders[r, j, g] == g_me for r, j in slots]
        late = g_me * 0
        for m, v in zip(own, names):
            late = jnp.where(m, v, late)
        early = late
        for m, v in zip(own[::-1], names[::-1]):
            early = jnp.where(m, v, early)
        picks[g, 0] = early
        picks[g, 1] = late

    def fill_and_send(c):
        def one(i, carry):
            g = torus_peer(g_me, groups, i)
            if c == 0:
                table(g)
            for k in range(CAP):
                b = picks[g, k]
                if c == 1:
                    sends[c][g, k, :, :qw] = pools[c][b]
                    sends[c][g, k, :, qw:] = prope[b]
                elif c == final:
                    sends[c][g, k, :piece] = pools[c][b]
                    sends[c][g, k, piece:] = pools[c + 1][b]
                else:
                    sends[c][g, k] = pools[c][b]
            plane_copy(c, g).start()
            return carry

        lax.fori_loop(1, groups, one, 0)

    def plane_copy(c, g):
        return pltpu.make_async_remote_copy(
            src_ref=sends[c].at[g],
            dst_ref=gots[c].at[g_me],
            send_sem=xy_send.at[c],
            recv_sem=xy_recv.at[c],
            device_id={"group": g},
            device_id_type=MESH,
        )

    def others(ref):
        return ref.at[pl.ds(1, groups - 1)]

    def plane_wait(c):
        pltpu.make_async_copy(others(gots[c]), others(gots[c]), xy_recv.at[c]).wait()

    def suffix_copy(h, way, layer, arriving):
        step = h + 1 if arriving else h
        origin = lax.rem(t_me + (tps - step if way == 0 else step), tps)
        ref = sufs[layer].at[pl.ds(pl.multiple_of(origin * rows, rows), rows)]
        if layer == 1:
            ref = ref.at[:, pl.ds(0, dc)]
        return pltpu.make_async_remote_copy(
            src_ref=ref,
            dst_ref=ref,
            send_sem=suf_send.at[h, way, layer],
            recv_sem=suf_recv.at[h, way, layer],
            device_id={"tp": (right, left)[way]},
            device_id_type=MESH,
        )

    last_hop = tps // 2 - 1

    def carried(h, way):
        return (0, 1) if h < last_hop else (way,)

    def suffix_send(h):
        for way in range(2):
            for layer in carried(h, way):
                suffix_copy(h, way, layer, False).start()

    def suffix_wait(h):
        for way in range(2):
            for layer in carried(h, way):
                suffix_copy(h, way, layer, True).wait_recv()

    def suffix_forward(h):
        suffix_wait(h - 1)
        suffix_send(h)

    for at in range(5):
        loads[at].wait()
    sufs[0][mine, hw : hw + rw] = jnp.concatenate(
        [srope[0].astype(F32), srope[1].astype(F32)], axis=1
    ).astype(BF16)
    pl.semaphore_wait(barrier, groups + 1)
    suffix_send(0)
    fill_and_send(0)

    loads[5].wait()
    loads[6].wait()
    held = prope.shape[0]
    low = lax.broadcasted_iota(jnp.int32, (held, 2 * dr), 1) < dr
    for j in range(piece // 2):
        x0 = prope_lanes[0, :, 2 * dr * j : 2 * dr * (j + 1)].astype(F32)
        x1 = prope_lanes[1, :, 2 * dr * j : 2 * dr * (j + 1)].astype(F32)
        prope_wide[:, 2 * j, :] = jnp.where(low, x0, pltpu.roll(x1, dr, 1))
        prope_wide[:, 2 * j + 1, :] = jnp.where(low, pltpu.roll(x0, dr, 1), x1)
    prope[...] = prope_wide[...].astype(BF16)
    fill_and_send(1)

    own = [holders[r, j, g_me] for r, j in slots]
    for s, (r, j) in enumerate(slots):
        rank = jnp.int32(0)
        for h in own[:s]:
            rank = jnp.where(h == own[s], 1, rank)
        ranks[r, j] = rank
    for c in range(5):
        for k in range(CAP):
            gots[c][g_me, k] = jnp.zeros(gots[c].shape[2:], BF16)

    lane = lax.broadcasted_iota(jnp.int32, (suffix, 2 * dr), 1)

    def head_rows(h, n):
        return pl.ds(pl.multiple_of(h * suffix, suffix), n * suffix)

    def absorb(layer):
        def one(hp, carry):
            for j in range(2):
                at = pl.ds(pl.multiple_of((hp * 2 + j) * dn, dn), dn)
                a = dot(qn[layer, :, at], wk[layer, hp * 2 + j]).astype(BF16)
                for r in range(requests):
                    to = head_rows(hp * 2 + j, 1)
                    part = a[r * suffix : (r + 1) * suffix]
                    if layer == 0:
                        absorbed0[r, to, :hw] = part[:, :hw]
                        absorbed0[r, to, hw + rw :] = part[:, hw:]
                    else:
                        absorbed1[r, to, :dc] = part
            at = pl.ds(pl.multiple_of(hp * rw, rw), rw)
            for r in range(requests):
                both = qr[layer, r * suffix : (r + 1) * suffix, at].astype(F32)
                swapped = pltpu.roll(both, dr, 1)
                for j in range(2):
                    to = head_rows(hp * 2 + j, 1)
                    values = swapped if j != layer else both
                    if layer == 0:
                        absorbed0[r, to, hw : hw + rw] = jnp.where(lane < dr, values, 0.0).astype(BF16)
                    else:
                        absorbed1[r, to, dc:] = jnp.where(lane >= dr, values, 0.0).astype(BF16)
            return carry

        lax.fori_loop(0, pairs, one, 0)

    def compact(c):
        def one(b, carry):
            for r in range(requests):
                at = pl.ds(pl.multiple_of(b * piece, piece), piece)
                source, rank = holders[r, b, g_me], ranks[r, b]
                into = keys[(0, 0, 0, 1, 1)[c]]
                to = pl.ds(places[c], widths[c])
                if c == final:
                    into[quarter, r, at, to] = gots[c][source, rank, :piece]
                    into[q_far, r, at, to] = gots[c][source, rank, piece:]
                else:
                    into[quarter, r, at, to] = gots[c][source, rank]
            return carry

        lax.fori_loop(0, blocks, one, 0)

    def part(c, q, r, at):
        return keys[(0, 0, 0, 1, 1)[c]].at[q, r, at, pl.ds(places[c], widths[c])]

    def ring_copy(ref, hop, unit, way):
        sems = ((hop1_send, hop1_recv), (hop2_send, hop2_recv))[hop]
        return pltpu.make_async_remote_copy(
            src_ref=ref,
            dst_ref=ref,
            send_sem=sems[0].at[unit, way],
            recv_sem=sems[1].at[unit, way],
            device_id={"tp": (right, left)[way]},
            device_id_type=MESH,
        )

    def hop1(c, r, way):
        return ring_copy(part(c, quarter, r, whole), 0, c * requests + r, way)

    def hop1_in(c, r, way):
        return ring_copy(part(c, (q_left, q_right)[way], r, whole), 0, c * requests + r, way)

    def hop2(c, r, way):
        ref = part(c, (q_left, q_right)[way], r, pl.ds(way * half, half))
        return ring_copy(ref, 1, c * requests + r, way)

    def hop2_in(c, r, way):
        ref = part(c, q_far, r, pl.ds(way * half, half))
        return ring_copy(ref, 1, c * requests + r, way)

    def ring_send(c, r):
        for way in range(2):
            hop1(c, r, way).start()

    def forward(c, r):
        for way in range(2):
            hop1_in(c, r, way).wait_recv()
            if c != final:
                hop2(c, r, way).start()

    def arrived(c, r):
        for way in range(2):
            hop2_in(c, r, way).wait_recv()

    def attend(layer, r, quarters, with_suffix, first, last):
        all_rows = heads * suffix
        suffix_rows = slice(r * suffix, (r + 1) * suffix)
        key_at = lax.broadcasted_iota(jnp.int32, (all_rows, seg), 1)
        live_prefix = key_at < prefix_blocks[r, g_me] * piece
        a = (absorbed0, absorbed1)[layer].at[r]
        if layer == 0:
            sides = (slice(0, hw), slice(hw + rw, dc + rw))
            terms = sides + (slice(hw, hw + rw),)
        else:
            sides = (slice(0, hw), slice(hw, dc))
            terms = sides + (slice(dc, dc + rw),)

        def score(k):
            return sum(dot_t(a[:, t], k[:, t]) for t in terms)

        scores = []
        for q in quarters:
            if layer == 1:
                keys[1][q, r, :, dc:] = keys[0][q, r, :, hw : hw + rw]
            scores.append(jnp.where(live_prefix, score(keys[layer].at[q, r]), -jnp.inf))
        values = [keys[layer].at[q, r] for q in quarters]
        if with_suffix:
            s = score(sufs[layer].at[suffix_rows])
            query_at = lax.rem(lax.broadcasted_iota(jnp.int32, s.shape, 0), suffix)
            live_suffix = lax.broadcasted_iota(jnp.int32, s.shape, 1) <= query_at
            scores.append(jnp.where(live_suffix, s, -jnp.inf))
            values.append(sufs[layer].at[suffix_rows])
        count = len(quarters)
        top = functools.reduce(jnp.maximum, scores[:count]).max(axis=1, keepdims=True)
        if with_suffix:
            top = jnp.maximum(top, scores[count].max(axis=1, keepdims=True))
        top = top * scale
        if not first:
            before = held_top[r]
            top = jnp.maximum(top, before)
            kept = jnp.exp2(before - top)
        probs = [jnp.exp2(s * scale - top) for s in scores]
        total = sum(probs[:count]).sum(axis=1, keepdims=True)
        if with_suffix:
            total = total + probs[count].sum(axis=1, keepdims=True)
        probs = [p.astype(BF16) for p in probs]
        contexts = [sum(dot(p, v[:, side]) for p, v in zip(probs, values)) for side in sides]
        if not first:
            total = total + held_total[r] * kept
            width = dc // len(sides)
            contexts = [
                c + held_context[r, :, i * width : (i + 1) * width] * kept
                for i, c in enumerate(contexts)
            ]
        if not last:
            held_top[r] = top
            held_total[r] = total
            for i, c in enumerate(contexts):
                held_context[r, :, i * c.shape[1] : (i + 1) * c.shape[1]] = c
            return
        inverse = 1.0 / total
        context = jnp.concatenate([(c * inverse).astype(BF16) for c in contexts], axis=1)
        for h in range(heads):
            out[layer, suffix_rows, h * dv : (h + 1) * dv] = dot(
                context[h * suffix : (h + 1) * suffix], wv[layer, h]
            ).astype(BF16)

    if last_hop > 1:
        suffix_forward(1)
    plane_wait(0)
    compact(0)
    ring_send(0, 0)
    ring_send(0, 1)
    loads[7].wait()
    fill_and_send(2)
    if last_hop > 2:
        suffix_forward(2)
    for at in (9, 10, 11):
        loads[at].wait()
    absorb(0)
    plane_wait(1)
    compact(1)
    ring_send(1, 0)
    ring_send(1, 1)
    suffix_forward(last_hop)
    forward(0, 0)
    forward(0, 1)
    loads[8].wait()
    fill_and_send(3)
    plane_wait(2)
    compact(2)
    ring_send(2, 0)
    ring_send(2, 1)
    forward(1, 0)
    forward(1, 1)
    loads[12].wait()
    loads[13].wait()
    fill_and_send(final)
    absorb(1)
    suffix_wait(last_hop)
    sufs[1][:, dc:] = sufs[0][:, hw : hw + rw]
    loads[14].wait()
    plane_wait(3)
    compact(3)
    forward(2, 0)
    forward(2, 1)
    ring_send(3, 0)
    ring_send(3, 1)
    for c in range(3):
        arrived(c, 0)
    attend(0, 0, range(QUARTERS), True, True, True)
    forward(3, 0)
    forward(3, 1)
    plane_wait(final)
    compact(final)
    ring_send(final, 0)
    ring_send(final, 1)
    for c in range(3):
        arrived(c, 1)
    attend(0, 1, range(QUARTERS), True, True, True)
    for r in range(requests):
        arrived(3, r)
        forward(final, r)
        attend(1, r, range(QUARTERS), True, True, True)

    for c in range(5):
        pltpu.make_async_copy(others(sends[c]), others(sends[c]), xy_send.at[c]).wait()
        for r in range(requests):
            for way in range(2):
                hop1(c, r, way).wait_send()
                if c != final:
                    hop2(c, r, way).wait_send()
    for h in range(last_hop + 1):
        for way in range(2):
            for layer in carried(h, way):
                suffix_copy(h, way, layer, False).wait_send()


def per_device(
    queries_nope,
    queries_rope,
    w_key,
    w_value,
    suffix_latent,
    suffix_rope,
    pool_latent,
    pool_rope,
    block_holders,
    block_ids,
    prefix_blocks,
):
    groups = lax.axis_size("group")
    tps = lax.axis_size("tp")
    requests, blocks = block_holders.shape[1:]
    layers, tokens = queries_nope.shape[:2]
    suffix = tokens // requests
    heads, dn, dc = w_key.shape[1:]
    dv = w_value.shape[3]
    dr = suffix_rope.shape[2]
    held, length = pool_latent.shape[1:3]
    piece = length // QUARTERS
    seg = blocks * piece
    rows = suffix_latent.shape[1]
    dims = (groups, tps, requests, blocks, suffix, heads, dc, dr, dn, dv)
    smem = pl.BlockSpec(memory_space=pltpu.SMEM)
    hbm = pl.BlockSpec(memory_space=pl.ANY)
    hw = dc // 2
    qw = dc // 4
    rw = 2 * dr
    final = 4
    qw = dc // 4
    rw = 2 * dr
    widths = (qw, qw + rw, hw, hw, hw)
    units = 5 * requests
    depths = (piece, piece, piece, piece, 2 * piece)
    landing = [pltpu.VMEM((groups, CAP, d, w), BF16) for d, w in zip(depths, widths)]
    hops = tps // 2
    return pl.pallas_call(
        functools.partial(kernel, dims),
        out_shape=pltpu.VMEM((layers, tokens, heads * dv), BF16),
        in_specs=[smem] * 3 + [hbm] * 8,
        out_specs=pl.BlockSpec(memory_space=pltpu.VMEM),
        scratch_shapes=[
            pltpu.VMEM(queries_nope.shape, BF16),
            pltpu.VMEM(queries_rope.shape, BF16),
            pltpu.VMEM(w_key.shape, BF16),
            pltpu.VMEM(w_value.shape, BF16),
            [pltpu.VMEM((held, piece, w), BF16) for w in (qw, qw, hw, hw, hw, hw)],
            pltpu.VMEM((layers, held, piece * dr), BF16),
            pltpu.VMEM((held, piece, 2 * dr), F32),
            pltpu.VMEM((held, piece, 2 * dr), BF16),
            pltpu.VMEM((layers, rows, dr), BF16),
            landing,
            landing,
            [pltpu.VMEM((QUARTERS, requests, seg, dc + rw), BF16) for _ in range(2)],
            [pltpu.VMEM((rows * tps, dc + rw), BF16) for _ in range(2)],
            pltpu.VMEM((requests, heads * suffix, dc + rw), BF16),
            pltpu.VMEM((requests, heads * suffix, dc + rw), BF16),
            pltpu.VMEM((requests, heads * suffix, 1), F32),
            pltpu.VMEM((requests, heads * suffix, 1), F32),
            pltpu.VMEM((requests, heads * suffix, dc), F32),
            pltpu.SMEM((groups, CAP), jnp.int32),
            pltpu.SMEM((requests, blocks), jnp.int32),
            pltpu.SemaphoreType.DMA((15,)),
            pltpu.SemaphoreType.DMA((5,)),
            pltpu.SemaphoreType.DMA((5,)),
            pltpu.SemaphoreType.DMA((hops, 2, 2)),
            pltpu.SemaphoreType.DMA((hops, 2, 2)),
            pltpu.SemaphoreType.DMA((units, 2)),
            pltpu.SemaphoreType.DMA((units, 2)),
            pltpu.SemaphoreType.DMA((units, 2)),
            pltpu.SemaphoreType.DMA((units, 2)),
        ],
        compiler_params=pltpu.CompilerParams(
            collective_id=0, has_side_effects=True, vmem_limit_bytes=56 * 1024 * 1024
        ),
        cost_estimate=pl.CostEstimate(
            flops=12_000_000_000, bytes_accessed=12_000_000, transcendentals=5_000_000
        ),
    )(
        block_holders.transpose(1, 2, 0),
        block_ids.transpose(1, 2, 0),
        prefix_blocks.T,
        queries_nope,
        queries_rope,
        w_key,
        w_value,
        suffix_latent,
        suffix_rope,
        pool_latent,
        pool_rope,
    )


def solution(mesh):
    in_specs = (
        P(None, "group", "tp"),
        P(None, "group", "tp"),
        P(None, "tp", None, None),
        P(None, "tp", None, None),
        P(None, ("group", "tp"), None),
        P(None, ("group", "tp"), None),
        P(None, "group", None, None),
        P(None, "group", None),
        P(),
        P(),
        P(),
    )
    out_specs = P(None, "group", "tp")
    return jax.shard_map(
        per_device, mesh=mesh, in_specs=in_specs, out_specs=out_specs, check_vma=False
    )
```

time: 86.9 us -> 70.4 us (0.81)
  the two profiles are of different devices: /device:TPU:1 before, /device:TPU:8 now
where the time goes in v3:
time: 70.4 us; the launch traced here: 70.2 us
  Pallas kernels  69.2 us (98%)
  local copies, waits for them, and re-layouts  0.97 us (1%)
    pallas_call x1, Pallas kernels, per_device(): pl.pallas_call(functools.partial(kernel, dims), out_shape=pltpu.VMEM((lay...  69.2 us

profile of v3, /device:TPU:8, one launch (start us, length us, event | category | flops | bytes accessed | tf_op | source)
XLA Modules:
  0.0 70.2 jit_solution(13222764942000200365)
XLA Ops:
  0.0 69.2 %shard_map.109 = bf16[2,256,1024]{2,1,0:T(8,128)(2,1)S(1)} custom-call(s32[2,16,32]{2,1,0:T(8,128)} %bitcast.3, s32[2,16,32]{2,1,0:T(8,128)} %bitcast.4, s32[2,32]{1,0:T(2,128)} %bitcast.5, bf16[2,256,1024]{2,1,0:T(8,128)(2,1)} %qn_in.1, bf16[2,256,512]{2,1,0:T(8,128)(2,1)} %qr_in.1, bf16[2,8,128,512]{3,2,1,0:T(8,128)(2,1)} %wk_in.1, ...), custom_call_target="tpu_custom_call" | custom-call | flops 12000000000 | bytes 12000000 | tf_op jit(solution)/shard_map/pallas_call | solution.py:522
  69.2 1.0 %copy.13 = bf16[2,256,1024]{2,1,0:T(8,128)(2,1)} copy(bf16[2,256,1024]{2,1,0:T(8,128)(2,1)S(1)} %shard_map.109) | data formatting | bytes 2097152

commit v4 on v3

--- a/solution.py
+++ b/solution.py
@@ -99,6 +99,7 @@
     qw = dc // 4
     rw = 2 * dr
     final = 4
+    doubled = 3
     scale = math.log2(math.e) / math.sqrt(dn + dr)
 
     first = pl.multiple_of(quarter * piece, piece)
@@ -122,8 +123,9 @@
         pltpu.make_async_copy(wk_in, wk, in_sem.at[10]),
         pltpu.make_async_copy(qr_in, qr, in_sem.at[11]),
         pltpu.make_async_copy(pool_in.at[1, :, tokens, pl.ds(hw, hw)], pools[4], in_sem.at[12]),
-        pltpu.make_async_copy(pool_in.at[1, :, far, pl.ds(hw, hw)], pools[5], in_sem.at[13]),
+        pltpu.make_async_copy(pool_in.at[1, :, far, pl.ds(hw, hw)], pools[6], in_sem.at[13]),
         pltpu.make_async_copy(wv_in, wv, in_sem.at[14]),
+        pltpu.make_async_copy(pool_in.at[1, :, far, pl.ds(0, hw)], pools[5], in_sem.at[15]),
     ]
     for load in loads:
         load.start()
@@ -164,9 +166,9 @@
                 if c == 1:
                     sends[c][g, k, :, :qw] = pools[c][b]
                     sends[c][g, k, :, qw:] = prope[b]
-                elif c == final:
+                elif c >= doubled:
                     sends[c][g, k, :piece] = pools[c][b]
-                    sends[c][g, k, piece:] = pools[c + 1][b]
+                    sends[c][g, k, piece:] = pools[c + 2][b]
                 else:
                     sends[c][g, k] = pools[c][b]
             plane_copy(c, g).start()
@@ -295,7 +297,7 @@
                 source, rank = holders[r, b, g_me], ranks[r, b]
                 into = keys[(0, 0, 0, 1, 1)[c]]
                 to = pl.ds(places[c], widths[c])
-                if c == final:
+                if c >= doubled:
                     into[quarter, r, at, to] = gots[c][source, rank, :piece]
                     into[q_far, r, at, to] = gots[c][source, rank, piece:]
                 else:
@@ -339,7 +341,7 @@
     def forward(c, r):
         for way in range(2):
             hop1_in(c, r, way).wait_recv()
-            if c != final:
+            if c < doubled:
                 hop2(c, r, way).start()
 
     def arrived(c, r):
@@ -430,6 +432,7 @@
     forward(0, 0)
     forward(0, 1)
     loads[8].wait()
+    loads[15].wait()
     fill_and_send(3)
     plane_wait(2)
     compact(2)
@@ -444,35 +447,37 @@
     suffix_wait(last_hop)
     sufs[1][:, dc:] = sufs[0][:, hw : hw + rw]
     loads[14].wait()
+    for r in range(requests):
+        attend(0, r, (quarter,), True, True, False)
     plane_wait(3)
     compact(3)
     forward(2, 0)
     forward(2, 1)
     ring_send(3, 0)
     ring_send(3, 1)
-    for c in range(3):
-        arrived(c, 0)
-    attend(0, 0, range(QUARTERS), True, True, True)
-    forward(3, 0)
-    forward(3, 1)
+    for r in range(requests):
+        attend(0, r, (q_left, q_right), False, False, False)
+    for r in range(requests):
+        for c in range(3):
+            arrived(c, r)
+        attend(0, r, (q_far,), False, False, True)
     plane_wait(final)
     compact(final)
     ring_send(final, 0)
     ring_send(final, 1)
-    for c in range(3):
-        arrived(c, 1)
-    attend(0, 1, range(QUARTERS), True, True, True)
     for r in range(requests):
-        arrived(3, r)
+        attend(1, r, (quarter, q_far), True, True, False)
+    for r in range(requests):
+        forward(3, r)
         forward(final, r)
-        attend(1, r, range(QUARTERS), True, True, True)
+        attend(1, r, (q_left, q_right), False, False, True)
 
     for c in range(5):
         pltpu.make_async_copy(others(sends[c]), others(sends[c]), xy_send.at[c]).wait()
         for r in range(requests):
             for way in range(2):
                 hop1(c, r, way).wait_send()
-                if c != final:
+                if c < doubled:
                     hop2(c, r, way).wait_send()
     for h in range(last_hop + 1):
         for way in range(2):
@@ -512,11 +517,12 @@
     qw = dc // 4
     rw = 2 * dr
     final = 4
+    doubled = 3
     qw = dc // 4
     rw = 2 * dr
     widths = (qw, qw + rw, hw, hw, hw)
     units = 5 * requests
-    depths = (piece, piece, piece, piece, 2 * piece)
+    depths = (piece, piece, piece, 2 * piece, 2 * piece)
     landing = [pltpu.VMEM((groups, CAP, d, w), BF16) for d, w in zip(depths, widths)]
     hops = tps // 2
     return pl.pallas_call(
@@ -529,7 +535,7 @@
             pltpu.VMEM(queries_rope.shape, BF16),
             pltpu.VMEM(w_key.shape, BF16),
             pltpu.VMEM(w_value.shape, BF16),
-            [pltpu.VMEM((held, piece, w), BF16) for w in (qw, qw, hw, hw, hw, hw)],
+            [pltpu.VMEM((held, piece, w), BF16) for w in (qw, qw, hw, hw, hw, hw, hw)],
             pltpu.VMEM((layers, held, piece * dr), BF16),
             pltpu.VMEM((held, piece, 2 * dr), F32),
             pltpu.VMEM((held, piece, 2 * dr), BF16),
@@ -545,7 +551,7 @@
             pltpu.VMEM((requests, heads * suffix, dc), F32),
             pltpu.SMEM((groups, CAP), jnp.int32),
             pltpu.SMEM((requests, blocks), jnp.int32),
-            pltpu.SemaphoreType.DMA((15,)),
+            pltpu.SemaphoreType.DMA((16,)),
             pltpu.SemaphoreType.DMA((5,)),
             pltpu.SemaphoreType.DMA((5,)),
             pltpu.SemaphoreType.DMA((hops, 2, 2)),

time: 70.4 us -> 70.4 us (level)
  no operation moved by 1% of the time
where the time goes in v4:
time: 70.4 us; the launch traced here: 69.7 us
  Pallas kernels  68.8 us (98%)
  local copies, waits for them, and re-layouts  0.97 us (1%)
    pallas_call x1, Pallas kernels, per_device(): pl.pallas_call(functools.partial(kernel, dims), out_shape=pltpu.VMEM((lay...  68.8 us

profile of v4, /device:TPU:8, one launch (start us, length us, event | category | flops | bytes accessed | tf_op | source)
XLA Modules:
  0.0 69.7 jit_solution(14094834891082609566)
XLA Ops:
  0.0 68.8 %shard_map.109 = bf16[2,256,1024]{2,1,0:T(8,128)(2,1)S(1)} custom-call(s32[2,16,32]{2,1,0:T(8,128)} %bitcast.3, s32[2,16,32]{2,1,0:T(8,128)} %bitcast.4, s32[2,32]{1,0:T(2,128)} %bitcast.5, bf16[2,256,1024]{2,1,0:T(8,128)(2,1)} %qn_in.1, bf16[2,256,512]{2,1,0:T(8,128)(2,1)} %qr_in.1, bf16[2,8,128,512]{3,2,1,0:T(8,128)(2,1)} %wk_in.1, ...), custom_call_target="tpu_custom_call" | custom-call | flops 12000000000 | bytes 12000000 | tf_op jit(solution)/shard_map/pallas_call | solution.py:528
  68.8 1.0 %copy.13 = bf16[2,256,1024]{2,1,0:T(8,128)(2,1)} copy(bf16[2,256,1024]{2,1,0:T(8,128)(2,1)S(1)} %shard_map.109) | data formatting | bytes 2097152
